TPU v7x, 128 devices: a whole 4x4x4 slice. The times are simulated.
128 devices in a mesh: dom: 64 (over z, y, x), tip: 2 (over core).
Axes of the slice: x: 4, y: 4, z: 4, core: 2. Of those that a mesh axis runs over, the one named last changes fastest.
Arguments:
- band_maps: bfloat16 [64, 1024, 1024], P('dom', None, 'tip')
- right_tips: float32 [64, 32, 1024], P('dom', None, 'tip'), may hold values from -1.5 to 1.5
- spikes: bfloat16 [64, 1024, 2048], P('dom', 'tip'), may hold values from -0.1875 to 0.1875
- local_parts: float32 [64, 32, 2048], P('dom', None, 'tip'), may hold values from -6 to 6
Outputs:
- interface: float32 [64, 32, 1024], P('dom', None, 'tip')
- interior: float32 [64, 32, 2048], P('dom', None, 'tip')
All inputs are finite; a program needn't handle non-finite values.
Results may differ from a plain program's by a relative error of at most 0.002.
Values may be sent and summed in bfloat16 or wider, within the bound.
A program may use at most 64 MiB of HBM per device.

v0:
```python
import jax
import jax.numpy as jnp
from jax import lax
from jax.sharding import PartitionSpec as P


def from_behind(value, axis, steps):
    count = lax.axis_size(axis)
    initial, last = (max(0, -steps), min(count, count - steps))
    return lax.ppermute(value, axis, [(source, source + steps) for source in range(initial, last)])


def on_device(band_maps, right_tips, spikes, local_parts):
    block = band_maps[0]
    tip_values = right_tips[0]
    domains = lax.axis_size("dom")
    current_map = block.astype(jnp.float32)
    stride = 1
    steps = (domains + stride - 1) // stride - 1

    def accumulate(total, piece):
        return total + jnp.dot(piece, current_map, precision=lax.Precision.HIGHEST)

    def advance(step, state):
        preceding_tips = from_behind(state, "dom", stride)
        return accumulate(tip_values, lax.all_gather(preceding_tips, "tip", axis=1, tiled=True))

    state = lax.fori_loop(0, steps, advance, tip_values)
    previous = from_behind(state.astype(jnp.bfloat16), "dom", 1)
    product = jnp.dot(previous, spikes[0], preferred_element_type=jnp.float32)
    share = lax.psum_scatter(product, "tip", scatter_dimension=1, tiled=True)
    interior = local_parts[0] - share
    return (state[None], interior[None])


def solution(mesh):
    return jax.shard_map(
        on_device,
        mesh=mesh,
        in_specs=(
            P("dom", None, "tip"),
            P("dom", None, "tip"),
            P("dom", "tip", None),
            P("dom", None, "tip"),
        ),
        out_specs=(P("dom", None, "tip"), P("dom", None, "tip")),
        check_vma=False,
    )
```

profile of v0, /device:TPU:121, one launch (start us, length us, event | category | flops | bytes accessed | tf_op | source)
XLA Modules:
  0.0 993.9 jit_solution(172877346333136132)
XLA Ops:
  11.1 897.5 %while.10 = (s32[]{:T(128)}, f32[32,512]{1,0:T(8,128)S(1)}, f32[1024,512]{1,0:T(8,128)}, f32[32,512]{1,0:T(8,128)S(1)}, s32[]{:T(128)}) while((s32[]{:T(128)}, f32[32,512]{1,0:T(8,128)S(1)}, f32[1024,512]{1,0:T(8,128)}, f32[32,512]{1,0:T(8,128)S(1)}, s32[]{:T(128)}) %tuple.27), condition=%wide.region_1.0_spmd, body=%wide.region_0.0_spmd.sunk | while | flops 201342976 | bytes 2818149 | solution.py:28
  39.5 5.2 collective-permute-done
  52.5 5.2 collective-permute-done
  78.6 5.2 collective-permute-done
  91.7 5.2 collective-permute-done
  117.8 5.2 collective-permute-done
  130.9 5.2 collective-permute-done
  157.0 5.2 collective-permute-done
  183.1 5.2 collective-permute-done
  196.2 5.2 collective-permute-done
  366.0 6.2 collective-permute-done
  379.4 8.0 collective-permute-done
  394.6 8.0 collective-permute-done
  409.7 8.0 collective-permute-done
  424.9 8.0 collective-permute-done
  440.1 8.0 collective-permute-done
  455.3 8.0 collective-permute-done
  470.4 8.0 collective-permute-done
  485.6 8.0 collective-permute-done
  500.8 8.0 collective-permute-done
  516.0 8.0 collective-permute-done
  531.1 8.0 collective-permute-done
  546.3 8.0 collective-permute-done
  561.5 8.0 collective-permute-done
  576.7 8.0 collective-permute-done
  591.8 8.0 collective-permute-done
  607.0 8.0 collective-permute-done
  622.2 8.0 collective-permute-done
  637.4 8.0 collective-permute-done
  652.5 8.0 collective-permute-done
  667.7 8.0 collective-permute-done
  682.9 8.0 collective-permute-done
  698.1 8.0 collective-permute-done
  713.2 8.0 collective-permute-done
  728.4 8.0 collective-permute-done
  743.6 8.0 collective-permute-done
  758.8 8.0 collective-permute-done
  773.9 8.0 collective-permute-done
  789.1 8.0 collective-permute-done
  804.3 8.0 collective-permute-done
  819.5 8.0 collective-permute-done
  834.6 8.0 collective-permute-done
  849.8 8.0 collective-permute-done
  865.0 8.0 collective-permute-done
  880.2 8.0 collective-permute-done
  895.3 8.0 collective-permute-done
  910.7 7.1 collective-permute-done.1
  918.9 66.5 %reduce-scatter.2.cloned.1.call-done = f32[32,1024]{1,0:T(8,128)} async-done(((f32[32,2048]{1,0:T(8,128)}), f32[32,1024]{1,0:T(8,128)}) %reduce-scatter.2.cloned.1.call-update) | async-done | bytes 131088 | tf_op jit(solution)/shard_map/reduce_scatter | solution.py:31
  (223 shorter events, 573.0 us)
Async XLA Ops:
  7.2 978.3 %reduce-scatter.2.cloned.1.call-start = ((), (), s32[]{:S(2)}) async-start(), calls=%async_computation.1 | async-start | bytes 393216 | tf_op jit(solution)/shard_map/reduce_scatter | solution.py:31
  24.5 7.1 collective-permute-start
  37.5 7.1 collective-permute-start
  50.6 7.1 collective-permute-start
  76.7 7.1 collective-permute-start
  89.8 7.1 collective-permute-start
  115.9 7.1 collective-permute-start
  129.0 7.1 collective-permute-start
  142.0 7.1 collective-permute-start
  155.1 7.1 collective-permute-start
  181.2 7.1 collective-permute-start
  364.1 8.1 collective-permute-start
  377.5 9.9 collective-permute-start
  392.6 9.9 collective-permute-start
  407.8 9.9 collective-permute-start
  423.0 9.9 collective-permute-start
  438.2 9.9 collective-permute-start
  453.3 9.9 collective-permute-start
  468.5 9.9 collective-permute-start
  483.7 9.9 collective-permute-start
  498.9 9.9 collective-permute-start
  514.0 9.9 collective-permute-start
  529.2 9.9 collective-permute-start
  544.4 9.9 collective-permute-start
  559.6 9.9 collective-permute-start
  574.7 9.9 collective-permute-start
  589.9 9.9 collective-permute-start
  605.1 9.9 collective-permute-start
  620.3 9.9 collective-permute-start
  635.4 9.9 collective-permute-start
  650.6 9.9 collective-permute-start
  665.8 9.9 collective-permute-start
  681.0 9.9 collective-permute-start
  696.1 9.9 collective-permute-start
  711.3 9.9 collective-permute-start
  726.5 9.9 collective-permute-start
  741.7 9.9 collective-permute-start
  756.8 9.9 collective-permute-start
  772.0 9.9 collective-permute-start
  787.2 9.9 collective-permute-start
  802.4 9.9 collective-permute-start
  817.5 9.9 collective-permute-start
  832.7 9.9 collective-permute-start
  847.9 9.9 collective-permute-start
  863.1 9.9 collective-permute-start
  878.2 9.9 collective-permute-start
  893.4 9.9 collective-permute-start
  908.6 9.1 collective-permute-start.1
  (21 other events, 1190.8 us)
Sparse Core Ops, SparseCore 0:
  919.1 66.3 reduce-scatter.1
where the time goes:
time: 1000 us; the launch traced here: 994 us
  waiting for transfers between devices  497 us (50%)
  matrix products  183 us (18%)
  blocking collectives  168 us (17%)
  starting transfers between devices  124 us (12%)
  between operations  14.1 us (1%)
    ppermute x64, waiting for transfers between devices, from_behind(): lax.ppermute(value, axis, [(source, source + steps) for source in range(i...  431 us
    dot_general x63, matrix products, accumulate(): return total + jnp.dot(piece, current_map, precision=lax.Precision.HIGHEST)  182 us
    all_gather x63, blocking collectives, advance(): lax.all_gather(preceding_tips, 'tip', axis=1, tiled=True)  168 us
    ppermute x64, starting transfers between devices, from_behind(): lax.ppermute(value, axis, [(source, source + steps) for source in range(i...  124 us
    reduce_scatter x1, waiting for transfers between devices, on_device(): share = lax.psum_scatter(product, 'tip', scatter_dimension=1, tiled=True)  66.5 us
  transfers between devices with their start and end apart: 65, of which 65 were waited for; matrix products, arithmetic and copies ran while one was open for 0% of the time, Pallas kernels for 0%

commit v1 on v0

v1 whole, which is shorter than its diff:
```python
import functools

import jax
import jax.numpy as jnp
from jax import lax
from jax.experimental import pallas as pl
from jax.experimental.pallas import tpu as pltpu
from jax.sharding import PartitionSpec as P

MESH = pl.DeviceIdType.MESH
RING = 4
CHAIN_ROWS = 2


def split_rows(value):
    high = value.astype(jnp.bfloat16)
    low = value - high.astype(jnp.float32)
    return jnp.concatenate([high.astype(jnp.float32), low], 0).astype(jnp.bfloat16)


def times_map(value, left, right):
    rows = value.shape[0]
    parts = split_rows(value)
    out = [jnp.dot(parts, half, preferred_element_type=jnp.float32) for half in (left, right)]
    return [piece[:rows] + piece[rows:] for piece in out]


def sweep(
    rows_total, maps_hbm, tips_ref, spikes_hbm, interface_ref, product_ref,
    maps, tips_out, tips_few, tips_many, few_in, many_in, many_out, states, prior, prior_many, full, spikes,
    local_sem, sib_send, sib_recv, link_send, link_recv, fwd_send, opp_recv,
    tip_send, tip_recv, wave_send, wave_recv, home_send, home_recv, side_send, side_recv,
):
    me, tip = lax.axis_index("dom"), lax.axis_index("tip")
    x, row = lax.rem(me, RING), lax.div(me, RING)
    other = 1 - tip
    base = me - x
    depth = maps_hbm.shape[1]
    half = maps_hbm.shape[2]
    cut = depth // 2
    width = spikes_hbm.shape[2] // 2
    chained = row < CHAIN_ROWS
    ringed = row >= CHAIN_ROWS
    last_chain = CHAIN_ROWS * RING - 1
    right, left = base + lax.rem(x + 1, RING), base + lax.rem(x + 3, RING)
    opposite = base + lax.rem(x + 2, RING)
    many = full.shape[0] // 2
    few = many // RING

    def remote(src, dst, send, recv, dom, to):
        return pltpu.make_async_remote_copy(
            src_ref=src, dst_ref=dst, send_sem=send, recv_sem=recv, device_id=(dom, to), device_id_type=MESH
        )

    barrier = pltpu.get_barrier_semaphore()

    def greet(dom, to):
        pl.semaphore_signal(barrier, inc=1, device_id=(dom, to), device_id_type=MESH)

    greet(me, other)

    @pl.when(chained)
    def _():
        @pl.when(me > 0)
        def _():
            greet(me - 1, tip)

    @pl.when(ringed)
    def _():
        for step in range(1, RING):
            for to in range(2):
                greet(base + lax.rem(x + step, RING), to)
        greet(jnp.where(row == CHAIN_ROWS, last_chain, me - RING), tip)

    own_map = pltpu.make_async_copy(maps_hbm.at[0], maps.at[x, tip], local_sem.at[0])
    own_map.start()
    own_columns = pl.ds(pl.multiple_of(tip * width, width), width)
    other_columns = pl.ds(pl.multiple_of(other * width, width), width)
    own_spikes = pltpu.make_async_copy(spikes_hbm.at[0, :, own_columns], spikes.at[tip], local_sem.at[1])
    own_spikes.start()
    for piece in range(2 * RING):
        tips_out[piece] = tips_ref[0, piece * few : (piece + 1) * few, :]

    @pl.when(chained)
    def _():
        pl.semaphore_wait(barrier, jnp.where(me == last_chain, 1 + RING, 2))

    @pl.when(ringed)
    def _():
        pl.semaphore_wait(barrier, jnp.where(row == rows_total - 1, 7, 8))

    pieces = [slice(0, cut), slice(cut, depth)]

    def sibling_map(step, part):
        slot = lax.rem(x + step, RING)
        block = maps.at[slot, tip, pieces[part]]
        return remote(block, block, sib_send.at[step, part], sib_recv.at[step, part], me, other)

    def sibling_map_arrives(step, part):
        slot = lax.rem(x + step, RING)
        block = maps.at[slot, other, pieces[part]]
        remote(block, block, sib_send.at[step, part], sib_recv.at[step, part], me, other).wait_recv()

    def own_sibling_map(part):
        src = maps_hbm.at[0, pieces[part]]
        return remote(src, maps.at[x, tip, pieces[part]], sib_send.at[0, part], sib_recv.at[0, part], me, other)

    spikes_out = remote(
        spikes_hbm.at[0, :, other_columns], spikes.at[tip], side_send.at[0], side_recv.at[0], me, other
    )

    @pl.when(chained)
    def _():
        for part in range(2):
            own_sibling_map(part).start()
        tip_rows = pl.ds(pl.multiple_of(other * many, many), many)
        tips_copy = remote(
            tips_ref.at[0, tip_rows, :], tips_many.at[tip], tip_send.at[0], tip_recv.at[0, 1], me, other
        )
        tips_copy.start()
        spikes_out.start()
        own_map.wait()
        for part in range(2):
            sibling_map_arrives(0, part)
        tips_copy.wait_recv()
        many_from = remote(many_in, many_in, wave_send.at[0], wave_recv.at[0], me, other)

        @pl.when(me > 0)
        def _():
            many_from.wait_recv()

        @pl.when(me == 0)
        def _():
            many_in[...] = jnp.zeros_like(many_in)

        own_rows = pl.ds(pl.multiple_of(tip * many, many), many)
        fresh = times_map(many_in[...], maps[x, 0], maps[x, 1])
        tips_many[tip] = tips_ref[0, own_rows, :]
        fresh = [fresh[h] + tips_many[h] for h in range(2)]

        @pl.when(me < last_chain)
        def _():
            for h in range(2):
                many_out[:, h * half : (h + 1) * half] = fresh[h]
            remote(many_out, many_in, wave_send.at[0], wave_recv.at[0], me + 1, tip).start()

        @pl.when(me == last_chain)
        def _():
            for piece in range(RING):
                for h in range(2):
                    states[piece, :, h * half : (h + 1) * half] = fresh[h][piece * few : (piece + 1) * few]
            for piece in range(RING):
                remote(
                    states.at[piece], few_in, home_send.at[piece, 0], wave_recv.at[1], last_chain + 1 + piece, tip
                ).start()

        to_sibling = remote(many_in, prior_many, side_send.at[1], side_recv.at[1], me, other)
        to_sibling.start()
        full[own_rows, :] = many_in[...]
        to_sibling.wait_recv()
        full[tip_rows, :] = prior_many[...]

        to_sibling.wait_send()
        tips_copy.wait_send()
        for part in range(2):
            own_sibling_map(part).wait_send()

        @pl.when(me < last_chain)
        def _():
            remote(many_out, many_in, wave_send.at[0], wave_recv.at[0], me, other).wait_send()

        @pl.when(me == last_chain)
        def _():
            for piece in range(RING):
                remote(
                    states.at[piece], few_in, home_send.at[piece, 0], wave_recv.at[1], last_chain + 1 + piece, tip
                ).wait_send()

    @pl.when(ringed)
    def _():
        def own_part(part, side):
            return remote(
                maps_hbm.at[0, pieces[part]], maps.at[x, tip, pieces[part]],
                link_send.at[side, part], link_recv.at[side, part], right if side == 0 else left, tip,
            )

        def neighbour_arrives(part, side):
            slot = lax.rem(x + (3 if side == 0 else 1), RING)
            block = maps.at[slot, tip, pieces[part]]
            remote(block, block, link_send.at[side, part], link_recv.at[side, part], right, tip).wait_recv()

        def forward(side):
            slot = lax.rem(x + (3 if side == 0 else 1), RING)
            block = maps.at[slot, tip, pieces[side]]
            return remote(block, block, fwd_send.at[side], opp_recv.at[side], right if side == 0 else left, tip)

        def opposite_arrives(side):
            block = maps.at[lax.rem(x + 2, RING), tip, pieces[side]]
            remote(block, block, fwd_send.at[side], opp_recv.at[side], right, tip).wait_recv()

        own_part(0, 0).start()
        own_part(1, 1).start()
        own_part(1, 0).start()
        own_part(0, 1).start()

        def tip_copy(step, to, number):
            dst_x = lax.rem(x + step, RING)
            return remote(
                tips_out.at[to * RING + dst_x], tips_few.at[x, tip],
                tip_send.at[number], tip_recv.at[step, jnp.where(to == tip, 0, 1)], base + dst_x, to,
            )

        partners = [(0, other), (1, tip), (1, other), (2, tip), (2, other), (3, tip), (3, other)]
        for number, (step, to) in enumerate(partners):
            tip_copy(step, to, number).start()
        tips_few[x, tip] = tips_out[tip * RING + x]
        for part in range(2):
            own_sibling_map(part).start()
        spikes_out.start()
        for part, side in ((0, 0), (1, 1)):
            neighbour_arrives(part, side)
            forward(side).start()
            sibling_map(3 if side == 0 else 1, part).start()
        for part, side in ((1, 0), (0, 1)):
            neighbour_arrives(part, side)
            sibling_map(3 if side == 0 else 1, part).start()
        for side in range(2):
            opposite_arrives(side)
            sibling_map(2, side).start()
        own_map.wait()
        for step in (0, 1, 3, 2):
            for part in range(2):
                sibling_map_arrives(step, part)
        for step, to in partners:
            remote(
                tips_few.at[0, 0], tips_few.at[0, 0], tip_send.at[0],
                tip_recv.at[step, jnp.where(to == tip, 0, 1)], me, other,
            ).wait_recv()

        mine = tip * RING + x

        def home_copy(step, to):
            src = few_in if step == 0 else states.at[step - 1]
            return remote(src, prior.at[mine], home_send.at[step, to], home_recv.at[mine], base + step, to)

        def send_home(step):
            for to in range(2):
                @pl.when(jnp.logical_or(x != step, tip != to))
                def _():
                    home_copy(step, to).start()

            @pl.when(x == step)
            def _():
                prior[mine] = few_in[...] if step == 0 else states[step - 1]

        onward = remote(states.at[RING - 1], few_in, wave_send.at[0], wave_recv.at[1], me + RING, tip)
        remote(few_in, few_in, wave_send.at[0], wave_recv.at[1], me, other).wait_recv()
        state = few_in[...]
        for step in range(RING):
            fresh = times_map(state, maps[step, 0], maps[step, 1])
            for h in range(2):
                states[step, :, h * half : (h + 1) * half] = fresh[h] + tips_few[step, h]
            state = states[step]

        @pl.when(row < rows_total - 1)
        def _():
            onward.start()

        for step in range(RING):
            send_home(step)
        for piece in range(2 * RING):
            @pl.when(piece != mine)
            def _():
                remote(
                    prior.at[piece], prior.at[piece], home_send.at[0, 0], home_recv.at[piece], me, other
                ).wait_recv()
        for piece in range(2 * RING):
            full[piece * few : (piece + 1) * few, :] = prior[piece]

        for part in range(2):
            for side in range(2):
                own_part(part, side).wait_send()
            own_sibling_map(part).wait_send()
            forward(part).wait_send()
            for step in range(1, RING):
                sibling_map(step, part).wait_send()
        for number, (step, to) in enumerate(partners):
            tip_copy(step, to, number).wait_send()

        @pl.when(row < rows_total - 1)
        def _():
            onward.wait_send()

        for step in range(RING):
            for to in range(2):
                @pl.when(jnp.logical_or(x != step, tip != to))
                def _():
                    home_copy(step, to).wait_send()

    own_spikes.wait()
    spikes_out.wait()
    count = full.shape[0]
    parts = split_rows(full[...])
    fresh = jnp.dot(parts, maps[x, tip], preferred_element_type=jnp.float32)
    interface_ref[0] = fresh[:count] + fresh[count:]
    middle = spikes.shape[1]
    product = jnp.dot(parts[:count, :middle], spikes[0], preferred_element_type=jnp.float32)
    product_ref[0] = product + jnp.dot(parts[:count, middle:], spikes[1], preferred_element_type=jnp.float32)


def on_device(band_maps, right_tips, spikes, local_parts):
    rows_total = lax.axis_size("dom") // RING
    _, depth, half = band_maps.shape
    count = right_tips.shape[1]
    many = count // 2
    few = many // RING
    _, spike_rows, spike_columns = spikes.shape
    width = spike_columns // 2
    f32, b16, dma = jnp.float32, jnp.bfloat16, pltpu.SemaphoreType.DMA
    interface, product = pl.pallas_call(
        functools.partial(sweep, rows_total),
        out_shape=(
            jax.ShapeDtypeStruct((1, count, half), f32),
            jax.ShapeDtypeStruct((1, count, width), f32),
        ),
        in_specs=[
            pl.BlockSpec(memory_space=pl.ANY),
            pl.BlockSpec(memory_space=pltpu.VMEM),
            pl.BlockSpec(memory_space=pl.ANY),
        ],
        out_specs=(pl.BlockSpec(memory_space=pltpu.VMEM),) * 2,
        scratch_shapes=[
            pltpu.VMEM((RING, 2, depth, half), b16),
            pltpu.VMEM((2 * RING, few, half), f32),
            pltpu.VMEM((RING, 2, few, half), f32),
            pltpu.VMEM((2, many, half), f32),
            pltpu.VMEM((few, depth), f32),
            pltpu.VMEM((many, depth), f32),
            pltpu.VMEM((many, depth), f32),
            pltpu.VMEM((RING, few, depth), f32),
            pltpu.VMEM((2 * RING, few, depth), f32),
            pltpu.VMEM((many, depth), f32),
            pltpu.VMEM((count, depth), f32),
            pltpu.VMEM((2, spike_rows, width), b16),
            dma((2,)),
            dma((RING, 2)),
            dma((RING, 2)),
            dma((2, 2)),
            dma((2, 2)),
            dma((2,)),
            dma((2,)),
            dma((2 * RING - 1,)),
            dma((RING, 2)),
            dma((2,)),
            dma((2,)),
            dma((RING, 2)),
            dma((2 * RING,)),
            dma((2,)),
            dma((2,)),
        ],
        compiler_params=pltpu.CompilerParams(
            collective_id=0, has_side_effects=True, vmem_limit_bytes=40 << 20
        ),
    )(band_maps, right_tips, spikes)
    return right_tips + interface, local_parts - product


def solution(mesh):
    return jax.shard_map(
        on_device,
        mesh=mesh,
        in_specs=(
            P("dom", None, "tip"),
            P("dom", None, "tip"),
            P("dom", "tip", None),
            P("dom", None, "tip"),
        ),
        out_specs=(P("dom", None, "tip"), P("dom", None, "tip")),
        check_vma=False,
    )
```

time: 1000 us -> 106 us (0.11)
  waiting for transfers between devices: 497 us -> 0 us
  matrix products: 183 us -> 0 us
  blocking collectives: 168 us -> 0 us
  starting transfers between devices: 124 us -> 0 us
  Pallas kernels: 0 us -> 100 us
  between operations: 14.1 us -> 0.65 us
    ppermute x64 -> x0, waiting for transfers between devices: 431 us -> none  [from_behind(): lax.ppermute(value, axis, [(source, source + steps) for source in range(i...]
    dot_general x64 -> x0, matrix products: 183 us -> none  [the longest x63 182 us: accumulate(): return total + jnp.dot(piece, current_map, precision=lax.Precision.HIGHEST)]
    all_gather x63 -> x0, blocking collectives: 168 us -> none  [advance(): lax.all_gather(preceding_tips, 'tip', axis=1, tiled=True)]
    ppermute x64 -> x0, starting transfers between devices: 124 us -> none  [from_behind(): lax.ppermute(value, axis, [(source, source + steps) for source in range(i...]
    pallas_call x0 -> x1, Pallas kernels: none -> 100 us  [on_device(): pl.pallas_call(functools.partial(sweep, rows_total), out_shape=(jax.Shape...]
    reduce_scatter x1 -> x0, waiting for transfers between devices: 66.5 us -> none  [on_device(): share = lax.psum_scatter(product, 'tip', scatter_dimension=1, tiled=True)]
  transfers between devices with their start and end apart: 65 -> 0, of which waited for: 65 -> 0; matrix products, arithmetic and copies ran while one was open for 0% -> 0% of each run, Pallas kernels for 0% -> 0%
where the time goes in v1:
time: 106 us
  Pallas kernels  100 us (94%)
  local copies, waits for them, and re-layouts  3.65 us (3%)
  other arithmetic  1.31 us (1%)
    pallas_call x1, Pallas kernels, on_device(): pl.pallas_call(functools.partial(sweep, rows_total), out_shape=(jax.Shape...  100 us
    unnamed x8, local copies, waits for them, and re-layouts  3.65 us

profile of v1, /device:TPU:121, one launch (start us, length us, event | category | flops | bytes accessed | tf_op | source)
XLA Modules:
  0.0 105.6 jit_solution(12357818281457058086)
XLA Ops:
  0.6 0.0 copy-start
  0.6 1.6 %copy-done = bf16[1,512,2048]{2,1,0:T(8,128)(2,1)S(1)} copy-done((bf16[1,512,2048]{2,1,0:T(8,128)(2,1)S(1)}, bf16[1,512,2048]{2,1,0:T(8,128)(2,1)}, u32[]{:S(2)}) %copy-start) | copy-done | bytes 2097176
  2.2 0.0 copy-start.1
  2.2 1.2 %copy-done.1 = bf16[1,1024,512]{2,1,0:T(8,128)(2,1)S(1)} copy-done((bf16[1,1024,512]{2,1,0:T(8,128)(2,1)S(1)}, bf16[1,1024,512]{2,1,0:T(8,128)(2,1)}, u32[]{:S(2)}) %copy-start.1) | copy-done | bytes 1048600
  3.4 0.0 copy-start.2
  3.5 0.8 copy-done.2
  4.3 0.0 copy-start.3
  4.3 100.0 %shard_map.59 = (f32[1,32,512]{2,1,0:T(8,128)S(1)}, f32[1,32,1024]{2,1,0:T(8,128)S(1)}) custom-call(bf16[1,1024,512]{2,1,0:T(8,128)(2,1)S(1)} %copy-done.1, f32[1,32,512]{2,1,0:T(8,128)S(1)} %copy-done.2, bf16[1,512,2048]{2,1,0:T(8,128)(2,1)S(1)} %copy-done), custom_call_target="tpu_custom_call" | custom-call | tf_op jit(solution)/shard_map/pallas_call | solution.py:320
  104.3 0.6 add.3
  105.0 0.0 copy-done.3
  105.0 0.7 sub.3
Async XLA Ops:
  0.6 1.6 %copy-start = (bf16[1,512,2048]{2,1,0:T(8,128)(2,1)S(1)}, bf16[1,512,2048]{2,1,0:T(8,128)(2,1)}, u32[]{:S(2)}) copy-start(bf16[1,512,2048]{2,1,0:T(8,128)(2,1)} %spikes_hbm.1) | copy-start | bytes 6291460
  2.2 1.2 %copy-start.1 = (bf16[1,1024,512]{2,1,0:T(8,128)(2,1)S(1)}, bf16[1,1024,512]{2,1,0:T(8,128)(2,1)}, u32[]{:S(2)}) copy-start(bf16[1,1024,512]{2,1,0:T(8,128)(2,1)} %maps_hbm.1) | copy-start | bytes 3145732
  3.4 0.8 copy-start.2
  4.3 100.7 %copy-start.3 = (f32[1,32,1024]{2,1,0:T(8,128)S(1)}, f32[1,32,1024]{2,1,0:T(8,128)}, u32[]{:S(2)}) copy-start(f32[1,32,1024]{2,1,0:T(8,128)} %param.7) | copy-start | bytes 393220

commit v2 on v1

--- a/solution.py
+++ b/solution.py
@@ -10,6 +10,7 @@
 MESH = pl.DeviceIdType.MESH
 RING = 4
 CHAIN_ROWS = 2
+PRODUCT_ROW = 4
 
 
 def split_rows(value):
@@ -25,9 +26,35 @@
     return [piece[:rows] + piece[rows:] for piece in out]
 
 
+def four_maps(maps, tip, high, low):
+    depth, half = maps.shape[2], maps.shape[3]
+    block = min(256, depth)
+
+    for turn, step in enumerate((2, 1, 0)):
+        def rows_of(index, _, turn=turn, step=step):
+            rows = pl.ds(pl.multiple_of(index * block, block), block)
+            total = None
+            for h in range(2):
+                lhs = maps[step, h, rows, :]
+                if turn == 0:
+                    factors = [maps[3, tip, h * half : (h + 1) * half, :]]
+                else:
+                    factors = [ref[(turn - 1) % 2, h * half : (h + 1) * half, :] for ref in (high, low)]
+                for factor in factors:
+                    term = jnp.dot(lhs, factor, preferred_element_type=jnp.float32)
+                    total = term if total is None else total + term
+            top = total.astype(jnp.bfloat16)
+            high[turn % 2, rows, :] = top
+            low[turn % 2, rows, :] = (total - top.astype(jnp.float32)).astype(jnp.bfloat16)
+            return 0
+
+        lax.fori_loop(0, depth // block, rows_of, 0)
+
+
 def sweep(
-    rows_total, maps_hbm, tips_ref, spikes_hbm, interface_ref, product_ref,
-    maps, tips_out, tips_few, tips_many, few_in, many_in, many_out, states, prior, prior_many, full, spikes,
+    rows_total, maps_hbm, tips_hbm, spikes_hbm, interface_ref, product_ref,
+    maps, tips_ref, tips_out, tips_both, tips_few, tips_many, few_in, pair_in, columns_in, columns_out, eight, local,
+    high, low, many_in, many_out, states, prior, prior_many, full, spikes,
     local_sem, sib_send, sib_recv, link_send, link_recv, fwd_send, opp_recv,
     tip_send, tip_recv, wave_send, wave_recv, home_send, home_recv, side_send, side_recv,
 ):
@@ -70,7 +97,12 @@
         for step in range(1, RING):
             for to in range(2):
                 greet(base + lax.rem(x + step, RING), to)
-        greet(jnp.where(row == CHAIN_ROWS, last_chain, me - RING), tip)
+        before = jnp.where(row == CHAIN_ROWS, last_chain, me - RING)
+        greet(before, tip)
+
+        @pl.when(row >= PRODUCT_ROW)
+        def _():
+            greet(before, other)
 
     own_map = pltpu.make_async_copy(maps_hbm.at[0], maps.at[x, tip], local_sem.at[0])
     own_map.start()
@@ -78,8 +110,13 @@
     other_columns = pl.ds(pl.multiple_of(other * width, width), width)
     own_spikes = pltpu.make_async_copy(spikes_hbm.at[0, :, own_columns], spikes.at[tip], local_sem.at[1])
     own_spikes.start()
-    for piece in range(2 * RING):
-        tips_out[piece] = tips_ref[0, piece * few : (piece + 1) * few, :]
+    own_tips = pltpu.make_async_copy(tips_hbm.at[0], tips_ref, local_sem.at[2])
+    own_tips.start()
+    own_tips.wait()
+    for piece in range(RING):
+        for to in range(2):
+            start = to * many + piece * few
+            tips_out[piece, to * few : (to + 1) * few, :] = tips_ref[start : start + few, :]
 
     @pl.when(chained)
     def _():
@@ -87,7 +124,8 @@
 
     @pl.when(ringed)
     def _():
-        pl.semaphore_wait(barrier, jnp.where(row == rows_total - 1, 7, 8))
+        after = jnp.where(row == rows_total - 1, 0, jnp.where(row >= PRODUCT_ROW - 1, 2, 1))
+        pl.semaphore_wait(barrier, 2 * RING - 1 + after)
 
     pieces = [slice(0, cut), slice(cut, depth)]
 
@@ -115,7 +153,7 @@
             own_sibling_map(part).start()
         tip_rows = pl.ds(pl.multiple_of(other * many, many), many)
         tips_copy = remote(
-            tips_ref.at[0, tip_rows, :], tips_many.at[tip], tip_send.at[0], tip_recv.at[0, 1], me, other
+            tips_ref.at[tip_rows, :], tips_many.at[tip], tip_send.at[0], tip_recv.at[0, 1], me, other
         )
         tips_copy.start()
         spikes_out.start()
@@ -123,42 +161,52 @@
         for part in range(2):
             sibling_map_arrives(0, part)
         tips_copy.wait_recv()
-        many_from = remote(many_in, many_in, wave_send.at[0], wave_recv.at[0], me, other)
-
-        @pl.when(me > 0)
-        def _():
-            many_from.wait_recv()
+
+        def many_send(h, dom):
+            return remote(many_out.at[h], many_in.at[h], wave_send.at[h], wave_recv.at[h], dom, tip)
+
+        own_rows = pl.ds(pl.multiple_of(tip * many, many), many)
+        tips_many[tip] = tips_ref[own_rows, :]
 
         @pl.when(me == 0)
         def _():
             many_in[...] = jnp.zeros_like(many_in)
 
-        own_rows = pl.ds(pl.multiple_of(tip * many, many), many)
-        fresh = times_map(many_in[...], maps[x, 0], maps[x, 1])
-        tips_many[tip] = tips_ref[0, own_rows, :]
-        fresh = [fresh[h] + tips_many[h] for h in range(2)]
-
-        @pl.when(me < last_chain)
-        def _():
+        total = [None, None]
+        for k in range(2):
+            @pl.when(me > 0)
+            def _():
+                remote(many_in.at[k], many_in.at[k], wave_send.at[k], wave_recv.at[k], me, other).wait_recv()
+
+            parts = split_rows(many_in[k])
             for h in range(2):
-                many_out[:, h * half : (h + 1) * half] = fresh[h]
-            remote(many_out, many_in, wave_send.at[0], wave_recv.at[0], me + 1, tip).start()
+                term = jnp.dot(parts, maps[x, h, k * half : (k + 1) * half, :], preferred_element_type=jnp.float32)
+                total[h] = term if k == 0 else total[h] + term
+                if k == 1:
+                    fresh = total[h][:many] + total[h][many:] + tips_many[h]
+                    many_out[h] = fresh
+
+                    @pl.when(me < last_chain)
+                    def _():
+                        many_send(h, me + 1).start()
 
         @pl.when(me == last_chain)
         def _():
             for piece in range(RING):
                 for h in range(2):
-                    states[piece, :, h * half : (h + 1) * half] = fresh[h][piece * few : (piece + 1) * few]
+                    states[piece, :, h * half : (h + 1) * half] = many_out[h, piece * few : (piece + 1) * few, :]
             for piece in range(RING):
                 remote(
-                    states.at[piece], few_in, home_send.at[piece, 0], wave_recv.at[1], last_chain + 1 + piece, tip
+                    states.at[piece], few_in, home_send.at[piece, 0], wave_recv.at[2], last_chain + 1 + piece, tip
                 ).start()
 
         to_sibling = remote(many_in, prior_many, side_send.at[1], side_recv.at[1], me, other)
         to_sibling.start()
-        full[own_rows, :] = many_in[...]
+        for h in range(2):
+            full[own_rows, h * half : (h + 1) * half] = many_in[h]
         to_sibling.wait_recv()
-        full[tip_rows, :] = prior_many[...]
+        for h in range(2):
+            full[tip_rows, h * half : (h + 1) * half] = prior_many[h]
 
         to_sibling.wait_send()
         tips_copy.wait_send()
@@ -167,13 +215,14 @@
 
         @pl.when(me < last_chain)
         def _():
-            remote(many_out, many_in, wave_send.at[0], wave_recv.at[0], me, other).wait_send()
+            for h in range(2):
+                many_send(h, me + 1).wait_send()
 
         @pl.when(me == last_chain)
         def _():
             for piece in range(RING):
                 remote(
-                    states.at[piece], few_in, home_send.at[piece, 0], wave_recv.at[1], last_chain + 1 + piece, tip
+                    states.at[piece], few_in, home_send.at[piece, 0], wave_recv.at[2], last_chain + 1 + piece, tip
                 ).wait_send()
 
     @pl.when(ringed)
@@ -206,14 +255,14 @@
         def tip_copy(step, to, number):
             dst_x = lax.rem(x + step, RING)
             return remote(
-                tips_out.at[to * RING + dst_x], tips_few.at[x, tip],
+                tips_out.at[dst_x], tips_both.at[x, tip],
                 tip_send.at[number], tip_recv.at[step, jnp.where(to == tip, 0, 1)], base + dst_x, to,
             )
 
         partners = [(0, other), (1, tip), (1, other), (2, tip), (2, other), (3, tip), (3, other)]
         for number, (step, to) in enumerate(partners):
             tip_copy(step, to, number).start()
-        tips_few[x, tip] = tips_out[tip * RING + x]
+        tips_both[x, tip] = tips_out[x]
         for part in range(2):
             own_sibling_map(part).start()
         spikes_out.start()
@@ -233,7 +282,7 @@
                 sibling_map_arrives(step, part)
         for step, to in partners:
             remote(
-                tips_few.at[0, 0], tips_few.at[0, 0], tip_send.at[0],
+                tips_both.at[0, 0], tips_both.at[0, 0], tip_send.at[0],
                 tip_recv.at[step, jnp.where(to == tip, 0, 1)], me, other,
             ).wait_recv()
 
@@ -253,21 +302,99 @@
             def _():
                 prior[mine] = few_in[...] if step == 0 else states[step - 1]
 
-        onward = remote(states.at[RING - 1], few_in, wave_send.at[0], wave_recv.at[1], me + RING, tip)
-        remote(few_in, few_in, wave_send.at[0], wave_recv.at[1], me, other).wait_recv()
-        state = few_in[...]
-        for step in range(RING):
+        def next_state(step, state):
             fresh = times_map(state, maps[step, 0], maps[step, 1])
             for h in range(2):
                 states[step, :, h * half : (h + 1) * half] = fresh[h] + tips_few[step, h]
-            state = states[step]
-
-        @pl.when(row < rows_total - 1)
-        def _():
-            onward.start()
+            return states[step]
+
+        def own_of(pair):
+            return jnp.where(tip == 0, pair[:few], pair[few:])
 
         for step in range(RING):
-            send_home(step)
+            for h in range(2):
+                tips_few[step, h] = own_of(tips_both[step, h])
+
+        final_row = row == rows_total - 1
+        direct = row < PRODUCT_ROW
+
+        def onward_rows(to):
+            return remote(states.at[RING - 1], few_in, wave_send.at[to], wave_recv.at[2], me + RING, tip)
+
+        def onward_pair(to):
+            return remote(
+                states.at[RING - 1], pair_in.at[tip], wave_send.at[to], wave_recv.at[3 + tip], me + RING, to
+            )
+
+        def onward_columns(to):
+            return remote(columns_out, columns_in.at[tip], wave_send.at[to], wave_recv.at[5 + tip], me + RING, to)
+
+        @pl.when(direct)
+        def _():
+            remote(few_in, few_in, wave_send.at[0], wave_recv.at[2], me, other).wait_recv()
+            state = few_in[...]
+            for step in range(RING):
+                state = next_state(step, state)
+
+            @pl.when(row < PRODUCT_ROW - 1)
+            def _():
+                onward_rows(0).start()
+
+            @pl.when(jnp.logical_and(row == PRODUCT_ROW - 1, jnp.logical_not(final_row)))
+            def _():
+                for to in range(2):
+                    onward_pair(to).start()
+
+            for step in range(RING):
+                send_home(step)
+
+        @pl.when(jnp.logical_not(direct))
+        def _():
+            @pl.when(jnp.logical_not(final_row))
+            def _():
+                four_maps(maps, tip, high, low)
+                state = jnp.concatenate([tips_both[0, 0], tips_both[0, 1]], 1)
+                for step in (1, 2):
+                    fresh = times_map(state, maps[step, 0], maps[step, 1])
+                    state = jnp.concatenate([fresh[h] + tips_both[step, h] for h in range(2)], 1)
+                parts = split_rows(state)
+                fresh = jnp.dot(parts, maps[3, tip], preferred_element_type=jnp.float32)
+                local[...] = fresh[: 2 * few] + fresh[2 * few :] + tips_both[3, tip]
+
+            @pl.when(row == PRODUCT_ROW)
+            def _():
+                for core in range(2):
+                    remote(
+                        pair_in.at[core], pair_in.at[core], wave_send.at[0], wave_recv.at[3 + core], me, other
+                    ).wait_recv()
+                for core in range(2):
+                    eight[core * few : (core + 1) * few, :] = pair_in[core]
+
+            @pl.when(row > PRODUCT_ROW)
+            def _():
+                for core in range(2):
+                    remote(
+                        columns_in.at[core], columns_in.at[core], wave_send.at[0], wave_recv.at[5 + core], me, other
+                    ).wait_recv()
+                for core in range(2):
+                    eight[:, core * half : (core + 1) * half] = columns_in[core]
+
+            @pl.when(jnp.logical_not(final_row))
+            def _():
+                parts = split_rows(eight[...])
+                fresh = jnp.dot(parts, high[0], preferred_element_type=jnp.float32)
+                fresh = fresh + jnp.dot(parts, low[0], preferred_element_type=jnp.float32)
+                columns_out[...] = fresh[: 2 * few] + fresh[2 * few :] + local[...]
+                for to in range(2):
+                    onward_columns(to).start()
+
+            few_in[...] = own_of(eight[...])
+            send_home(0)
+            state = few_in[...]
+            for step in range(RING - 1):
+                state = next_state(step, state)
+                send_home(step + 1)
+
         for piece in range(2 * RING):
             @pl.when(piece != mine)
             def _():
@@ -287,9 +414,19 @@
         for number, (step, to) in enumerate(partners):
             tip_copy(step, to, number).wait_send()
 
-        @pl.when(row < rows_total - 1)
-        def _():
-            onward.wait_send()
+        @pl.when(row < PRODUCT_ROW - 1)
+        def _():
+            onward_rows(0).wait_send()
+
+        @pl.when(jnp.logical_and(row == PRODUCT_ROW - 1, jnp.logical_not(final_row)))
+        def _():
+            for to in range(2):
+                onward_pair(to).wait_send()
+
+        @pl.when(jnp.logical_and(row >= PRODUCT_ROW, jnp.logical_not(final_row)))
+        def _():
+            for to in range(2):
+                onward_columns(to).wait_send()
 
         for step in range(RING):
             for to in range(2):
@@ -324,25 +461,34 @@
             jax.ShapeDtypeStruct((1, count, width), f32),
         ),
         in_specs=[
-            pl.BlockSpec(memory_space=pl.ANY),
-            pl.BlockSpec(memory_space=pltpu.VMEM),
-            pl.BlockSpec(memory_space=pl.ANY),
+            pl.BlockSpec(memory_space=pltpu.HBM),
+            pl.BlockSpec(memory_space=pltpu.HBM),
+            pl.BlockSpec(memory_space=pltpu.HBM),
         ],
         out_specs=(pl.BlockSpec(memory_space=pltpu.VMEM),) * 2,
         scratch_shapes=[
             pltpu.VMEM((RING, 2, depth, half), b16),
-            pltpu.VMEM((2 * RING, few, half), f32),
+            pltpu.VMEM((count, half), f32),
+            pltpu.VMEM((RING, 2 * few, half), f32),
+            pltpu.VMEM((RING, 2, 2 * few, half), f32),
             pltpu.VMEM((RING, 2, few, half), f32),
             pltpu.VMEM((2, many, half), f32),
             pltpu.VMEM((few, depth), f32),
-            pltpu.VMEM((many, depth), f32),
-            pltpu.VMEM((many, depth), f32),
+            pltpu.VMEM((2, few, depth), f32),
+            pltpu.VMEM((2, 2 * few, half), f32),
+            pltpu.VMEM((2 * few, half), f32),
+            pltpu.VMEM((2 * few, depth), f32),
+            pltpu.VMEM((2 * few, half), f32),
+            pltpu.VMEM((2, depth, half), b16),
+            pltpu.VMEM((2, depth, half), b16),
+            pltpu.VMEM((2, many, half), f32),
+            pltpu.VMEM((2, many, half), f32),
             pltpu.VMEM((RING, few, depth), f32),
             pltpu.VMEM((2 * RING, few, depth), f32),
-            pltpu.VMEM((many, depth), f32),
+            pltpu.VMEM((2, many, half), f32),
             pltpu.VMEM((count, depth), f32),
             pltpu.VMEM((2, spike_rows, width), b16),
-            dma((2,)),
+            dma((3,)),
             dma((RING, 2)),
             dma((RING, 2)),
             dma((2, 2)),
@@ -352,14 +498,14 @@
             dma((2 * RING - 1,)),
             dma((RING, 2)),
             dma((2,)),
-            dma((2,)),
+            dma((7,)),
             dma((RING, 2)),
             dma((2 * RING,)),
             dma((2,)),
             dma((2,)),
         ],
         compiler_params=pltpu.CompilerParams(
-            collective_id=0, has_side_effects=True, vmem_limit_bytes=40 << 20
+            collective_id=0, has_side_effects=True, vmem_limit_bytes=48 << 20
         ),
     )(band_maps, right_tips, spikes)
     return right_tips + interface, local_parts - product

time: 106 us -> 96.1 us (0.907)
  Pallas kernels: 100 us -> 90.1 us
    pallas_call x1, Pallas kernels: 100 us -> 90.1 us  [on_device(): pl.pallas_call(functools.partial(sweep, rows_total), out_shape=(jax.Shape...]
where the time goes in v2:
time: 96.1 us; the launch traced here: 95.7 us
  Pallas kernels  90.1 us (94%)
  local copies, waits for them, and re-layouts  3.65 us (4%)
  other arithmetic  1.31 us (1%)
    pallas_call x1, Pallas kernels, on_device(): pl.pallas_call(functools.partial(sweep, rows_total), out_shape=(jax.Shape...  90.1 us
    unnamed x8, local copies, waits for them, and re-layouts  3.65 us

profile of v2, /device:TPU:121, one launch (start us, length us, event | category | flops | bytes accessed | tf_op | source)
XLA Modules:
  0.0 95.7 jit_solution(17869920835678568822)
XLA Ops:
  0.6 0.0 copy-start
  0.6 1.6 %copy-done = bf16[1,512,2048]{2,1,0:T(8,128)(2,1)S(1)} copy-done((bf16[1,512,2048]{2,1,0:T(8,128)(2,1)S(1)}, bf16[1,512,2048]{2,1,0:T(8,128)(2,1)}, u32[]{:S(2)}) %copy-start) | copy-done | bytes 2097176
  2.2 0.0 copy-start.1
  2.2 1.2 %copy-done.1 = bf16[1,1024,512]{2,1,0:T(8,128)(2,1)S(1)} copy-done((bf16[1,1024,512]{2,1,0:T(8,128)(2,1)S(1)}, bf16[1,1024,512]{2,1,0:T(8,128)(2,1)}, u32[]{:S(2)}) %copy-start.1) | copy-done | bytes 1048600
  3.4 0.0 copy-start.2
  3.5 0.8 copy-done.2
  4.3 0.0 copy-start.3
  4.3 90.1 %shard_map.59 = (f32[1,32,512]{2,1,0:T(8,128)S(1)}, f32[1,32,1024]{2,1,0:T(8,128)S(1)}) custom-call(bf16[1,1024,512]{2,1,0:T(8,128)(2,1)S(1)} %copy-done.1, f32[1,32,512]{2,1,0:T(8,128)S(1)} %copy-done.2, bf16[1,512,2048]{2,1,0:T(8,128)(2,1)S(1)} %copy-done), custom_call_target="tpu_custom_call" | custom-call | tf_op jit(solution)/shard_map/pallas_call | solution.py:457
  94.4 0.6 add.3
  95.0 0.0 copy-done.3
  95.0 0.7 sub.3
Async XLA Ops:
  0.6 1.6 %copy-start = (bf16[1,512,2048]{2,1,0:T(8,128)(2,1)S(1)}, bf16[1,512,2048]{2,1,0:T(8,128)(2,1)}, u32[]{:S(2)}) copy-start(bf16[1,512,2048]{2,1,0:T(8,128)(2,1)} %spikes_hbm.1) | copy-start | bytes 6291460
  2.2 1.2 %copy-start.1 = (bf16[1,1024,512]{2,1,0:T(8,128)(2,1)S(1)}, bf16[1,1024,512]{2,1,0:T(8,128)(2,1)}, u32[]{:S(2)}) copy-start(bf16[1,1024,512]{2,1,0:T(8,128)(2,1)} %maps_hbm.1) | copy-start | bytes 3145732
  3.4 0.8 copy-start.2
  4.3 90.7 %copy-start.3 = (f32[1,32,1024]{2,1,0:T(8,128)S(1)}, f32[1,32,1024]{2,1,0:T(8,128)}, u32[]{:S(2)}) copy-start(f32[1,32,1024]{2,1,0:T(8,128)} %param.7) | copy-start | bytes 393220

commit v3 on v2

--- a/solution.py
+++ b/solution.py
@@ -9,8 +9,8 @@
 
 MESH = pl.DeviceIdType.MESH
 RING = 4
-CHAIN_ROWS = 2
-PRODUCT_ROW = 4
+CHAIN_ROWS = 3
+PRODUCT_ROW = 5
 
 
 def split_rows(value):
@@ -92,6 +92,10 @@
         def _():
             greet(me - 1, tip)
 
+        @pl.when(me == 1)
+        def _():
+            greet(0, other)
+
     @pl.when(ringed)
     def _():
         for step in range(1, RING):
@@ -120,7 +124,7 @@
 
     @pl.when(chained)
     def _():
-        pl.semaphore_wait(barrier, jnp.where(me == last_chain, 1 + RING, 2))
+        pl.semaphore_wait(barrier, jnp.where(me == last_chain, 1 + RING, jnp.where(me == 0, 3, 2)))
 
     @pl.when(ringed)
     def _():
@@ -147,8 +151,17 @@
         spikes_hbm.at[0, :, other_columns], spikes.at[tip], side_send.at[0], side_recv.at[0], me, other
     )
 
+    def first_rows(to):
+        rows = slice(to * many, (to + 1) * many)
+        return remote(tips_ref.at[rows, :], many_in.at[tip], wave_send.at[to], wave_recv.at[tip], 1, to)
+
     @pl.when(chained)
     def _():
+        @pl.when(me == 0)
+        def _():
+            for to in range(2):
+                first_rows(to).start()
+
         for part in range(2):
             own_sibling_map(part).start()
         tip_rows = pl.ds(pl.multiple_of(other * many, many), many)
@@ -186,7 +199,7 @@
                     fresh = total[h][:many] + total[h][many:] + tips_many[h]
                     many_out[h] = fresh
 
-                    @pl.when(me < last_chain)
+                    @pl.when(jnp.logical_and(me > 0, me < last_chain))
                     def _():
                         many_send(h, me + 1).start()
 
@@ -213,7 +226,12 @@
         for part in range(2):
             own_sibling_map(part).wait_send()
 
-        @pl.when(me < last_chain)
+        @pl.when(me == 0)
+        def _():
+            for to in range(2):
+                first_rows(to).wait_send()
+
+        @pl.when(jnp.logical_and(me > 0, me < last_chain))
         def _():
             for h in range(2):
                 many_send(h, me + 1).wait_send()
@@ -505,7 +523,7 @@
             dma((2,)),
         ],
         compiler_params=pltpu.CompilerParams(
-            collective_id=0, has_side_effects=True, vmem_limit_bytes=48 << 20
+            collective_id=0, has_side_effects=True, vmem_limit_bytes=60 << 20
         ),
     )(band_maps, right_tips, spikes)
     return right_tips + interface, local_parts - product

time: 96.1 us -> 95.3 us (level)
  local copies, waits for them, and re-layouts: 3.65 us -> 0.01 us
  other arithmetic: 1.31 us -> 3.05 us
    unnamed x8 -> x4, local copies, waits for them, and re-layouts: 3.65 us -> 0.01 us
where the time goes in v3:
time: 95.3 us; the launch traced here: 94.7 us
  Pallas kernels  91 us (95%)
  other arithmetic  3.05 us (3%)
    pallas_call x1, Pallas kernels, on_device(): pl.pallas_call(functools.partial(sweep, rows_total), out_shape=(jax.Shape...  91 us

profile of v3, /device:TPU:121, one launch (start us, length us, event | category | flops | bytes accessed | tf_op | source)
XLA Modules:
  0.0 94.7 jit_solution(750405777280600361)
XLA Ops:
  0.6 0.0 copy-start
  0.6 0.0 copy-start.1
  0.7 91.0 %shard_map.59 = (f32[1,32,512]{2,1,0:T(8,128)}, f32[1,32,1024]{2,1,0:T(8,128)}) custom-call(bf16[1,1024,512]{2,1,0:T(8,128)(2,1)} %maps_hbm.1, f32[1,32,512]{2,1,0:T(8,128)} %tips_hbm.1, bf16[1,512,2048]{2,1,0:T(8,128)(2,1)} %spikes_hbm.1), custom_call_target="tpu_custom_call" | custom-call | tf_op jit(solution)/shard_map/pallas_call | solution.py:475
  91.7 0.0 copy-done
  91.7 1.5 %add.3 = f32[1,32,512]{2,1,0:T(8,128)} add(f32[1,32,512]{2,1,0:T(8,128)S(1)} %copy-done, f32[1,32,512]{2,1,0:T(8,128)} %get-tuple-element.4) | non-fusion elementwise | flops 16384 | bytes 196608 | tf_op jit(solution)/shard_map/add | solution.py:529
  93.2 0.0 copy-done.1
  93.2 1.6 %sub.3 = f32[1,32,1024]{2,1,0:T(8,128)} subtract(f32[1,32,1024]{2,1,0:T(8,128)S(1)} %copy-done.1, f32[1,32,1024]{2,1,0:T(8,128)} %get-tuple-element.5) | non-fusion elementwise | flops 32768 | bytes 393216 | tf_op jit(solution)/shard_map/sub | solution.py:529
Async XLA Ops:
  0.6 91.0 %copy-start = (f32[1,32,512]{2,1,0:T(8,128)S(1)}, f32[1,32,512]{2,1,0:T(8,128)}, u32[]{:S(2)}) copy-start(f32[1,32,512]{2,1,0:T(8,128)} %tips_hbm.1) | copy-start | bytes 196612
  0.6 92.5 %copy-start.1 = (f32[1,32,1024]{2,1,0:T(8,128)S(1)}, f32[1,32,1024]{2,1,0:T(8,128)}, u32[]{:S(2)}) copy-start(f32[1,32,1024]{2,1,0:T(8,128)} %param.7) | copy-start | bytes 393220

commit v4 on v3

--- a/solution.py
+++ b/solution.py
@@ -53,9 +53,9 @@
 
 def sweep(
     rows_total, maps_hbm, tips_hbm, spikes_hbm, interface_ref, product_ref,
-    maps, tips_ref, tips_out, tips_both, tips_few, tips_many, few_in, pair_in, columns_in, columns_out, eight, local,
+    maps, tips_ref, tips_out, tips_both, tips_few, tips_many, few_in, pair_in, columns_in, columns_out, local,
     high, low, many_in, many_out, states, prior, prior_many, full, spikes,
-    local_sem, sib_send, sib_recv, link_send, link_recv, fwd_send, opp_recv,
+    local_sem, sib_send, sib_recv, quarter_send, quarter_recv, link_send, link_recv, fwd_send, opp_recv,
     tip_send, tip_recv, wave_send, wave_recv, home_send, home_recv, side_send, side_recv,
 ):
     me, tip = lax.axis_index("dom"), lax.axis_index("tip")
@@ -256,14 +256,27 @@
             block = maps.at[slot, tip, pieces[part]]
             remote(block, block, link_send.at[side, part], link_recv.at[side, part], right, tip).wait_recv()
 
-        def forward(side):
+        def quarter(side, k):
+            return slice(side * cut + k * (cut // 2), side * cut + (k + 1) * (cut // 2))
+
+        def forward(side, k):
             slot = lax.rem(x + (3 if side == 0 else 1), RING)
-            block = maps.at[slot, tip, pieces[side]]
-            return remote(block, block, fwd_send.at[side], opp_recv.at[side], right if side == 0 else left, tip)
-
-        def opposite_arrives(side):
-            block = maps.at[lax.rem(x + 2, RING), tip, pieces[side]]
-            remote(block, block, fwd_send.at[side], opp_recv.at[side], right, tip).wait_recv()
+            block = maps.at[slot, tip, quarter(side, k)]
+            return remote(
+                block, block, fwd_send.at[side, k], opp_recv.at[side, k], right if side == 0 else left, tip
+            )
+
+        def opposite_arrives(side, k):
+            block = maps.at[lax.rem(x + 2, RING), tip, quarter(side, k)]
+            remote(block, block, fwd_send.at[side, k], opp_recv.at[side, k], right, tip).wait_recv()
+
+        def sibling_quarter(side, k):
+            block = maps.at[lax.rem(x + 2, RING), tip, quarter(side, k)]
+            return remote(block, block, quarter_send.at[side, k], quarter_recv.at[side, k], me, other)
+
+        def sibling_quarter_arrives(side, k):
+            block = maps.at[lax.rem(x + 2, RING), other, quarter(side, k)]
+            remote(block, block, quarter_send.at[side, k], quarter_recv.at[side, k], me, other).wait_recv()
 
         own_part(0, 0).start()
         own_part(1, 1).start()
@@ -286,18 +299,23 @@
         spikes_out.start()
         for part, side in ((0, 0), (1, 1)):
             neighbour_arrives(part, side)
-            forward(side).start()
+            for k in range(2):
+                forward(side, k).start()
             sibling_map(3 if side == 0 else 1, part).start()
         for part, side in ((1, 0), (0, 1)):
             neighbour_arrives(part, side)
             sibling_map(3 if side == 0 else 1, part).start()
-        for side in range(2):
-            opposite_arrives(side)
-            sibling_map(2, side).start()
+        for k in range(2):
+            for side in range(2):
+                opposite_arrives(side, k)
+                sibling_quarter(side, k).start()
         own_map.wait()
-        for step in (0, 1, 3, 2):
+        for step in (0, 1, 3):
             for part in range(2):
                 sibling_map_arrives(step, part)
+        for k in range(2):
+            for side in range(2):
+                sibling_quarter_arrives(side, k)
         for step, to in partners:
             remote(
                 tips_both.at[0, 0], tips_both.at[0, 0], tip_send.at[0],
@@ -386,27 +404,38 @@
                         pair_in.at[core], pair_in.at[core], wave_send.at[0], wave_recv.at[3 + core], me, other
                     ).wait_recv()
                 for core in range(2):
-                    eight[core * few : (core + 1) * few, :] = pair_in[core]
-
-            @pl.when(row > PRODUCT_ROW)
+                    for h in range(2):
+                        columns_in[h, core * few : (core + 1) * few, :] = pair_in[core, :, h * half : (h + 1) * half]
+
+            def columns_arrive(core):
+                remote(
+                    columns_in.at[core], columns_in.at[core], wave_send.at[0], wave_recv.at[5 + core], me, other
+                ).wait_recv()
+
+            @pl.when(final_row)
             def _():
                 for core in range(2):
-                    remote(
-                        columns_in.at[core], columns_in.at[core], wave_send.at[0], wave_recv.at[5 + core], me, other
-                    ).wait_recv()
+                    columns_arrive(core)
+
+            @pl.when(jnp.logical_not(final_row))
+            def _():
+                total = local[...]
                 for core in range(2):
-                    eight[:, core * half : (core + 1) * half] = columns_in[core]
-
-            @pl.when(jnp.logical_not(final_row))
-            def _():
-                parts = split_rows(eight[...])
-                fresh = jnp.dot(parts, high[0], preferred_element_type=jnp.float32)
-                fresh = fresh + jnp.dot(parts, low[0], preferred_element_type=jnp.float32)
-                columns_out[...] = fresh[: 2 * few] + fresh[2 * few :] + local[...]
+                    @pl.when(row > PRODUCT_ROW)
+                    def _():
+                        columns_arrive(core)
+
+                    parts = split_rows(columns_in[core])
+                    for factor in (high, low):
+                        rows = factor[0, core * half : (core + 1) * half, :]
+                        fresh = jnp.dot(parts, rows, preferred_element_type=jnp.float32)
+                        total = total + fresh[: 2 * few] + fresh[2 * few :]
+                columns_out[...] = total
                 for to in range(2):
                     onward_columns(to).start()
 
-            few_in[...] = own_of(eight[...])
+            for h in range(2):
+                few_in[:, h * half : (h + 1) * half] = own_of(columns_in[h])
             send_home(0)
             state = few_in[...]
             for step in range(RING - 1):
@@ -426,8 +455,10 @@
             for side in range(2):
                 own_part(part, side).wait_send()
             own_sibling_map(part).wait_send()
-            forward(part).wait_send()
-            for step in range(1, RING):
+            for k in range(2):
+                forward(part, k).wait_send()
+                sibling_quarter(part, k).wait_send()
+            for step in (1, 3):
                 sibling_map(step, part).wait_send()
         for number, (step, to) in enumerate(partners):
             tip_copy(step, to, number).wait_send()
@@ -495,7 +526,6 @@
             pltpu.VMEM((2, few, depth), f32),
             pltpu.VMEM((2, 2 * few, half), f32),
             pltpu.VMEM((2 * few, half), f32),
-            pltpu.VMEM((2 * few, depth), f32),
             pltpu.VMEM((2 * few, half), f32),
             pltpu.VMEM((2, depth, half), b16),
             pltpu.VMEM((2, depth, half), b16),
@@ -511,8 +541,10 @@
             dma((RING, 2)),
             dma((2, 2)),
             dma((2, 2)),
-            dma((2,)),
-            dma((2,)),
+            dma((2, 2)),
+            dma((2, 2)),
+            dma((2, 2)),
+            dma((2, 2)),
             dma((2 * RING - 1,)),
             dma((RING, 2)),
             dma((2,)),
@@ -523,7 +555,7 @@
             dma((2,)),
         ],
         compiler_params=pltpu.CompilerParams(
-            collective_id=0, has_side_effects=True, vmem_limit_bytes=60 << 20
+            collective_id=0, has_side_effects=True, vmem_limit_bytes=53 << 20
         ),
     )(band_maps, right_tips, spikes)
     return right_tips + interface, local_parts - product

time: 95.3 us -> 94.8 us (level)
  other arithmetic: 3.05 us -> 1.31 us
where the time goes in v4:
time: 94.8 us; the launch traced here: 94.3 us
  Pallas kernels  91.5 us (97%)
  other arithmetic  1.31 us (1%)
    pallas_call x1, Pallas kernels, on_device(): pl.pallas_call(functools.partial(sweep, rows_total), out_shape=(jax.Shape...  91.5 us

profile of v4, /device:TPU:121, one launch (start us, length us, event | category | flops | bytes accessed | tf_op | source)
XLA Modules:
  0.0 94.3 jit_solution(5148135207309873283)
XLA Ops:
  0.6 0.0 copy-start
  0.6 0.8 copy-done
  1.5 0.0 copy-start.1
  1.5 91.5 %shard_map.59 = (f32[1,32,512]{2,1,0:T(8,128)S(1)}, f32[1,32,1024]{2,1,0:T(8,128)S(1)}) custom-call(bf16[1,1024,512]{2,1,0:T(8,128)(2,1)} %maps_hbm.1, f32[1,32,512]{2,1,0:T(8,128)S(1)} %copy-done, bf16[1,512,2048]{2,1,0:T(8,128)(2,1)} %spikes_hbm.1), custom_call_target="tpu_custom_call" | custom-call | tf_op jit(solution)/shard_map/pallas_call | solution.py:506
  93.0 0.6 add.3
  93.6 0.0 copy-done.1
  93.6 0.7 sub.3
Async XLA Ops:
  0.6 0.8 copy-start
  1.5 92.2 %copy-start.1 = (f32[1,32,1024]{2,1,0:T(8,128)S(1)}, f32[1,32,1024]{2,1,0:T(8,128)}, u32[]{:S(2)}) copy-start(f32[1,32,1024]{2,1,0:T(8,128)} %param.7) | copy-start | bytes 393220

commit v5 on v4

--- a/solution.py
+++ b/solution.py
@@ -10,7 +10,7 @@
 MESH = pl.DeviceIdType.MESH
 RING = 4
 CHAIN_ROWS = 3
-PRODUCT_ROW = 5
+PRODUCT_ROW = 4
 
 
 def split_rows(value):
@@ -27,28 +27,20 @@
 
 
 def four_maps(maps, tip, high, low):
-    depth, half = maps.shape[2], maps.shape[3]
-    block = min(256, depth)
-
+    half = maps.shape[3]
+    block = min(256, half)
     for turn, step in enumerate((2, 1, 0)):
-        def rows_of(index, _, turn=turn, step=step):
-            rows = pl.ds(pl.multiple_of(index * block, block), block)
-            total = None
-            for h in range(2):
-                lhs = maps[step, h, rows, :]
-                if turn == 0:
-                    factors = [maps[3, tip, h * half : (h + 1) * half, :]]
-                else:
-                    factors = [ref[(turn - 1) % 2, h * half : (h + 1) * half, :] for ref in (high, low)]
-                for factor in factors:
-                    term = jnp.dot(lhs, factor, preferred_element_type=jnp.float32)
-                    total = term if total is None else total + term
+        factor = jnp.concatenate([maps[step, 0], maps[step, 1]], 1)
+        for start in range(0, half, block):
+            columns = slice(start, start + block)
+            if turn == 0:
+                total = jnp.dot(factor, maps[3, tip, :, columns], preferred_element_type=jnp.float32)
+            else:
+                total = jnp.dot(factor, high[(turn - 1) % 2, :, columns], preferred_element_type=jnp.float32)
+                total += jnp.dot(factor, low[(turn - 1) % 2, :, columns], preferred_element_type=jnp.float32)
             top = total.astype(jnp.bfloat16)
-            high[turn % 2, rows, :] = top
-            low[turn % 2, rows, :] = (total - top.astype(jnp.float32)).astype(jnp.bfloat16)
-            return 0
-
-        lax.fori_loop(0, depth // block, rows_of, 0)
+            high[turn % 2, :, columns] = top
+            low[turn % 2, :, columns] = (total - top.astype(jnp.float32)).astype(jnp.bfloat16)
 
 
 def sweep(
@@ -116,12 +108,6 @@
     own_spikes.start()
     own_tips = pltpu.make_async_copy(tips_hbm.at[0], tips_ref, local_sem.at[2])
     own_tips.start()
-    own_tips.wait()
-    for piece in range(RING):
-        for to in range(2):
-            start = to * many + piece * few
-            tips_out[piece, to * few : (to + 1) * few, :] = tips_ref[start : start + few, :]
-
     @pl.when(chained)
     def _():
         pl.semaphore_wait(barrier, jnp.where(me == last_chain, 1 + RING, jnp.where(me == 0, 3, 2)))
@@ -153,7 +139,7 @@
 
     def first_rows(to):
         rows = slice(to * many, (to + 1) * many)
-        return remote(tips_ref.at[rows, :], many_in.at[tip], wave_send.at[to], wave_recv.at[tip], 1, to)
+        return remote(tips_hbm.at[0, rows, :], many_in.at[tip], wave_send.at[to], wave_recv.at[tip], 1, to)
 
     @pl.when(chained)
     def _():
@@ -162,6 +148,7 @@
             for to in range(2):
                 first_rows(to).start()
 
+        own_tips.wait()
         for part in range(2):
             own_sibling_map(part).start()
         tip_rows = pl.ds(pl.multiple_of(other * many, many), many)
@@ -282,6 +269,12 @@
         own_part(1, 1).start()
         own_part(1, 0).start()
         own_part(0, 1).start()
+
+        own_tips.wait()
+        for piece in range(RING):
+            for to in range(2):
+                start = to * many + piece * few
+                tips_out[piece, to * few : (to + 1) * few, :] = tips_ref[start : start + few, :]
 
         def tip_copy(step, to, number):
             dst_x = lax.rem(x + step, RING)
@@ -419,18 +412,15 @@
 
             @pl.when(jnp.logical_not(final_row))
             def _():
-                total = local[...]
-                for core in range(2):
-                    @pl.when(row > PRODUCT_ROW)
-                    def _():
+                @pl.when(row > PRODUCT_ROW)
+                def _():
+                    for core in range(2):
                         columns_arrive(core)
 
-                    parts = split_rows(columns_in[core])
-                    for factor in (high, low):
-                        rows = factor[0, core * half : (core + 1) * half, :]
-                        fresh = jnp.dot(parts, rows, preferred_element_type=jnp.float32)
-                        total = total + fresh[: 2 * few] + fresh[2 * few :]
-                columns_out[...] = total
+                parts = split_rows(jnp.concatenate([columns_in[0], columns_in[1]], 1))
+                fresh = jnp.dot(parts, high[0], preferred_element_type=jnp.float32)
+                fresh = fresh + jnp.dot(parts, low[0], preferred_element_type=jnp.float32)
+                columns_out[...] = fresh[: 2 * few] + fresh[2 * few :] + local[...]
                 for to in range(2):
                     onward_columns(to).start()
 

time: 94.8 us -> 92.8 us (0.979)
  Pallas kernels: 91.5 us -> 89.5 us
    pallas_call x1, Pallas kernels: 91.5 us -> 89.5 us  [on_device(): pl.pallas_call(functools.partial(sweep, rows_total), out_shape=(jax.Shape...]
where the time goes in v5:
time: 92.8 us; the launch traced here: 92.3 us
  Pallas kernels  89.5 us (96%)
  other arithmetic  1.31 us (1%)
    pallas_call x1, Pallas kernels, on_device(): pl.pallas_call(functools.partial(sweep, rows_total), out_shape=(jax.Shape...  89.5 us

profile of v5, /device:TPU:121, one launch (start us, length us, event | category | flops | bytes accessed | tf_op | source)
XLA Modules:
  0.0 92.3 jit_solution(7529185173080652574)
XLA Ops:
  0.6 0.0 copy-start
  0.6 0.8 copy-done
  1.5 0.0 copy-start.1
  1.5 89.5 %shard_map.59 = (f32[1,32,512]{2,1,0:T(8,128)S(1)}, f32[1,32,1024]{2,1,0:T(8,128)S(1)}) custom-call(bf16[1,1024,512]{2,1,0:T(8,128)(2,1)} %maps_hbm.1, f32[1,32,512]{2,1,0:T(8,128)S(1)} %copy-done, bf16[1,512,2048]{2,1,0:T(8,128)(2,1)} %spikes_hbm.1), custom_call_target="tpu_custom_call" | custom-call | tf_op jit(solution)/shard_map/pallas_call | solution.py:496
  91.0 0.6 add.3
  91.6 0.0 copy-done.1
  91.6 0.7 sub.3
Async XLA Ops:
  0.6 0.8 copy-start
  1.5 90.1 %copy-start.1 = (f32[1,32,1024]{2,1,0:T(8,128)S(1)}, f32[1,32,1024]{2,1,0:T(8,128)}, u32[]{:S(2)}) copy-start(f32[1,32,1024]{2,1,0:T(8,128)} %param.7) | copy-start | bytes 393220

commit v6 on v5

--- a/solution.py
+++ b/solution.py
@@ -9,8 +9,9 @@
 
 MESH = pl.DeviceIdType.MESH
 RING = 4
-CHAIN_ROWS = 3
-PRODUCT_ROW = 4
+CHAIN_ROWS = 2
+HELPED_ROWS = 2
+PRODUCT_ROW = 6
 
 
 def split_rows(value):
@@ -47,7 +48,8 @@
     rows_total, maps_hbm, tips_hbm, spikes_hbm, interface_ref, product_ref,
     maps, tips_ref, tips_out, tips_both, tips_few, tips_many, few_in, pair_in, columns_in, columns_out, local,
     high, low, many_in, many_out, states, prior, prior_many, full, spikes,
-    local_sem, sib_send, sib_recv, quarter_send, quarter_recv, link_send, link_recv, fwd_send, opp_recv,
+    local_sem, sib_send, sib_recv, quarter_send, quarter_recv, relay, relay_send, relay_recv, relay_sib_send, relay_sib_recv,
+    link_send, link_recv, fwd_send, opp_recv,
     tip_send, tip_recv, wave_send, wave_recv, home_send, home_recv, side_send, side_recv,
 ):
     me, tip = lax.axis_index("dom"), lax.axis_index("tip")
@@ -60,6 +62,11 @@
     width = spikes_hbm.shape[2] // 2
     chained = row < CHAIN_ROWS
     ringed = row >= CHAIN_ROWS
+    helped = jnp.logical_and(ringed, row < CHAIN_ROWS + HELPED_ROWS)
+    alone = row >= CHAIN_ROWS + HELPED_ROWS
+    helper = jnp.logical_and(chained, row >= CHAIN_ROWS - HELPED_ROWS)
+    mirrored = (2 * CHAIN_ROWS - 1 - row) * RING
+    relayed = maps_hbm.shape[1] // 4
     last_chain = CHAIN_ROWS * RING - 1
     right, left = base + lax.rem(x + 1, RING), base + lax.rem(x + 3, RING)
     opposite = base + lax.rem(x + 2, RING)
@@ -87,6 +94,10 @@
         @pl.when(me == 1)
         def _():
             greet(0, other)
+
+        @pl.when(helper)
+        def _():
+            greet(mirrored + x, tip)
 
     @pl.when(ringed)
     def _():
@@ -115,14 +126,9 @@
     @pl.when(ringed)
     def _():
         after = jnp.where(row == rows_total - 1, 0, jnp.where(row >= PRODUCT_ROW - 1, 2, 1))
-        pl.semaphore_wait(barrier, 2 * RING - 1 + after)
+        pl.semaphore_wait(barrier, 2 * RING - 1 + after + jnp.where(helped, 1, 0))
 
     pieces = [slice(0, cut), slice(cut, depth)]
-
-    def sibling_map(step, part):
-        slot = lax.rem(x + step, RING)
-        block = maps.at[slot, tip, pieces[part]]
-        return remote(block, block, sib_send.at[step, part], sib_recv.at[step, part], me, other)
 
     def sibling_map_arrives(step, part):
         slot = lax.rem(x + step, RING)
@@ -140,6 +146,25 @@
     def first_rows(to):
         rows = slice(to * many, (to + 1) * many)
         return remote(tips_hbm.at[0, rows, :], many_in.at[tip], wave_send.at[to], wave_recv.at[tip], 1, to)
+
+    def relay_rows(k):
+        start = depth - relayed + k * (relayed // 2)
+        return slice(start, start + relayed // 2)
+
+    def to_relay(k):
+        src = maps_hbm.at[0, relay_rows(k)]
+        return remote(src, relay.at[k], relay_send.at[0, k], relay_recv.at[0, k], mirrored + x, tip)
+
+    def from_relay(step, k):
+        dst = maps.at[x, tip, relay_rows(k)]
+        dom = mirrored + lax.rem(x + step, RING)
+        return remote(relay.at[k], dst, relay_send.at[step, k], relay_recv.at[step, k], dom, tip)
+
+    def pass_on():
+        for k in range(2):
+            remote(relay.at[k], relay.at[k], relay_send.at[0, k], relay_recv.at[0, k], me, other).wait_recv()
+            for step in range(1, RING):
+                from_relay(step, k).start()
 
     @pl.when(chained)
     def _():
@@ -172,6 +197,10 @@
         def _():
             many_in[...] = jnp.zeros_like(many_in)
 
+        @pl.when(jnp.logical_and(helper, row == CHAIN_ROWS - 1))
+        def _():
+            pass_on()
+
         total = [None, None]
         for k in range(2):
             @pl.when(me > 0)
@@ -200,6 +229,10 @@
                     states.at[piece], few_in, home_send.at[piece, 0], wave_recv.at[2], last_chain + 1 + piece, tip
                 ).start()
 
+        @pl.when(jnp.logical_and(helper, row < CHAIN_ROWS - 1))
+        def _():
+            pass_on()
+
         to_sibling = remote(many_in, prior_many, side_send.at[1], side_recv.at[1], me, other)
         to_sibling.start()
         for h in range(2):
@@ -208,6 +241,12 @@
         for h in range(2):
             full[tip_rows, h * half : (h + 1) * half] = prior_many[h]
 
+        @pl.when(helper)
+        def _():
+            for k in range(2):
+                for step in range(1, RING):
+                    from_relay(step, k).wait_send()
+
         to_sibling.wait_send()
         tips_copy.wait_send()
         for part in range(2):
@@ -232,43 +271,103 @@
 
     @pl.when(ringed)
     def _():
-        def own_part(part, side):
-            return remote(
-                maps_hbm.at[0, pieces[part]], maps.at[x, tip, pieces[part]],
-                link_send.at[side, part], link_recv.at[side, part], right if side == 0 else left, tip,
-            )
-
-        def neighbour_arrives(part, side):
-            slot = lax.rem(x + (3 if side == 0 else 1), RING)
-            block = maps.at[slot, tip, pieces[part]]
-            remote(block, block, link_send.at[side, part], link_recv.at[side, part], right, tip).wait_recv()
-
-        def quarter(side, k):
-            return slice(side * cut + k * (cut // 2), side * cut + (k + 1) * (cut // 2))
-
-        def forward(side, k):
-            slot = lax.rem(x + (3 if side == 0 else 1), RING)
-            block = maps.at[slot, tip, quarter(side, k)]
-            return remote(
-                block, block, fwd_send.at[side, k], opp_recv.at[side, k], right if side == 0 else left, tip
-            )
-
-        def opposite_arrives(side, k):
-            block = maps.at[lax.rem(x + 2, RING), tip, quarter(side, k)]
-            remote(block, block, fwd_send.at[side, k], opp_recv.at[side, k], right, tip).wait_recv()
-
-        def sibling_quarter(side, k):
-            block = maps.at[lax.rem(x + 2, RING), tip, quarter(side, k)]
-            return remote(block, block, quarter_send.at[side, k], quarter_recv.at[side, k], me, other)
-
-        def sibling_quarter_arrives(side, k):
-            block = maps.at[lax.rem(x + 2, RING), other, quarter(side, k)]
-            remote(block, block, quarter_send.at[side, k], quarter_recv.at[side, k], me, other).wait_recv()
-
-        own_part(0, 0).start()
-        own_part(1, 1).start()
-        own_part(1, 0).start()
-        own_part(0, 1).start()
+        class Gather:
+            def __init__(self, count):
+                self.cut = count // 2
+
+            def rows(self, part, k=None):
+                if k is None:
+                    return slice(part * self.cut, (part + 1) * self.cut)
+                size = self.cut // 2
+                return slice(part * self.cut + k * size, part * self.cut + (k + 1) * size)
+
+            def own(self, part, side):
+                rows = self.rows(part)
+                return remote(
+                    maps_hbm.at[0, rows], maps.at[x, tip, rows],
+                    link_send.at[side, part], link_recv.at[side, part], right if side == 0 else left, tip,
+                )
+
+            def neighbour_arrives(self, part, side):
+                block = maps.at[lax.rem(x + (3 if side == 0 else 1), RING), tip, self.rows(part)]
+                remote(block, block, link_send.at[side, part], link_recv.at[side, part], right, tip).wait_recv()
+
+            def forward(self, side, k):
+                block = maps.at[lax.rem(x + (3 if side == 0 else 1), RING), tip, self.rows(side, k)]
+                dom = right if side == 0 else left
+                return remote(block, block, fwd_send.at[side, k], opp_recv.at[side, k], dom, tip)
+
+            def opposite_arrives(self, side, k):
+                block = maps.at[lax.rem(x + 2, RING), tip, self.rows(side, k)]
+                remote(block, block, fwd_send.at[side, k], opp_recv.at[side, k], right, tip).wait_recv()
+
+            def to_sibling(self, step, part):
+                block = maps.at[lax.rem(x + step, RING), tip, self.rows(part)]
+                return remote(block, block, sib_send.at[step, part], sib_recv.at[step, part], me, other)
+
+            def sibling_arrives(self, step, part):
+                block = maps.at[lax.rem(x + step, RING), other, self.rows(part)]
+                remote(block, block, sib_send.at[step, part], sib_recv.at[step, part], me, other).wait_recv()
+
+            def quarter_to_sibling(self, side, k):
+                block = maps.at[lax.rem(x + 2, RING), tip, self.rows(side, k)]
+                return remote(block, block, quarter_send.at[side, k], quarter_recv.at[side, k], me, other)
+
+            def sibling_quarter_arrives(self, side, k):
+                block = maps.at[lax.rem(x + 2, RING), other, self.rows(side, k)]
+                remote(block, block, quarter_send.at[side, k], quarter_recv.at[side, k], me, other).wait_recv()
+
+            def start(self):
+                for part, side in ((0, 0), (1, 1), (1, 0), (0, 1)):
+                    self.own(part, side).start()
+
+            def middle(self):
+                for part, side in ((0, 0), (1, 1)):
+                    self.neighbour_arrives(part, side)
+                    for k in range(2):
+                        self.forward(side, k).start()
+                    self.to_sibling(3 if side == 0 else 1, part).start()
+                for part, side in ((1, 0), (0, 1)):
+                    self.neighbour_arrives(part, side)
+                    self.to_sibling(3 if side == 0 else 1, part).start()
+
+            def last(self):
+                for k in range(2):
+                    for side in range(2):
+                        self.opposite_arrives(side, k)
+                        self.quarter_to_sibling(side, k).start()
+                for step in (1, 3):
+                    for part in range(2):
+                        self.sibling_arrives(step, part)
+                for k in range(2):
+                    for side in range(2):
+                        self.sibling_quarter_arrives(side, k)
+
+            def drain(self):
+                for part in range(2):
+                    for side in range(2):
+                        self.own(part, side).wait_send()
+                    for k in range(2):
+                        self.forward(part, k).wait_send()
+                        self.quarter_to_sibling(part, k).wait_send()
+                    for step in (1, 3):
+                        self.to_sibling(step, part).wait_send()
+
+        whole, rest = Gather(depth), Gather(depth - relayed)
+
+        def relayed_to_sibling(step, k):
+            block = maps.at[lax.rem(x + RING - step, RING), tip, relay_rows(k)]
+            return remote(block, block, relay_sib_send.at[step, k], relay_sib_recv.at[step, k], me, other)
+
+        @pl.when(helped)
+        def _():
+            for k in range(2):
+                to_relay(k).start()
+            rest.start()
+
+        @pl.when(alone)
+        def _():
+            whole.start()
 
         own_tips.wait()
         for piece in range(RING):
@@ -290,25 +389,29 @@
         for part in range(2):
             own_sibling_map(part).start()
         spikes_out.start()
-        for part, side in ((0, 0), (1, 1)):
-            neighbour_arrives(part, side)
+
+        @pl.when(alone)
+        def _():
+            whole.middle()
+            whole.last()
+
+        @pl.when(helped)
+        def _():
+            rest.middle()
             for k in range(2):
-                forward(side, k).start()
-            sibling_map(3 if side == 0 else 1, part).start()
-        for part, side in ((1, 0), (0, 1)):
-            neighbour_arrives(part, side)
-            sibling_map(3 if side == 0 else 1, part).start()
-        for k in range(2):
-            for side in range(2):
-                opposite_arrives(side, k)
-                sibling_quarter(side, k).start()
+                for step in range(1, RING):
+                    block = maps.at[lax.rem(x + RING - step, RING), tip, relay_rows(k)]
+                    remote(block, block, relay_send.at[step, k], relay_recv.at[step, k], me, other).wait_recv()
+                    relayed_to_sibling(step, k).start()
+            rest.last()
+            for k in range(2):
+                for step in range(1, RING):
+                    block = maps.at[lax.rem(x + RING - step, RING), other, relay_rows(k)]
+                    remote(block, block, relay_sib_send.at[step, k], relay_sib_recv.at[step, k], me, other).wait_recv()
+
         own_map.wait()
-        for step in (0, 1, 3):
-            for part in range(2):
-                sibling_map_arrives(step, part)
-        for k in range(2):
-            for side in range(2):
-                sibling_quarter_arrives(side, k)
+        for part in range(2):
+            sibling_map_arrives(0, part)
         for step, to in partners:
             remote(
                 tips_both.at[0, 0], tips_both.at[0, 0], tip_send.at[0],
@@ -441,15 +544,20 @@
         for piece in range(2 * RING):
             full[piece * few : (piece + 1) * few, :] = prior[piece]
 
+        @pl.when(alone)
+        def _():
+            whole.drain()
+
+        @pl.when(helped)
+        def _():
+            rest.drain()
+            for k in range(2):
+                to_relay(k).wait_send()
+                for step in range(1, RING):
+                    relayed_to_sibling(step, k).wait_send()
+
         for part in range(2):
-            for side in range(2):
-                own_part(part, side).wait_send()
             own_sibling_map(part).wait_send()
-            for k in range(2):
-                forward(part, k).wait_send()
-                sibling_quarter(part, k).wait_send()
-            for step in (1, 3):
-                sibling_map(step, part).wait_send()
         for number, (step, to) in enumerate(partners):
             tip_copy(step, to, number).wait_send()
 
@@ -531,6 +639,11 @@
             dma((RING, 2)),
             dma((2, 2)),
             dma((2, 2)),
+            pltpu.VMEM((2, depth // 8, half), b16),
+            dma((RING, 2)),
+            dma((RING, 2)),
+            dma((RING, 2)),
+            dma((RING, 2)),
             dma((2, 2)),
             dma((2, 2)),
             dma((2, 2)),

time: 92.8 us -> 91.7 us (0.988)
  Pallas kernels: 89.5 us -> 88.4 us
    pallas_call x1, Pallas kernels: 89.5 us -> 88.4 us  [on_device(): pl.pallas_call(functools.partial(sweep, rows_total), out_shape=(jax.Shape...]
where the time goes in v6:
time: 91.7 us; the launch traced here: 91.2 us
  Pallas kernels  88.4 us (96%)
  other arithmetic  1.31 us (1%)
    pallas_call x1, Pallas kernels, on_device(): pl.pallas_call(functools.partial(sweep, rows_total), out_shape=(jax.Shape...  88.4 us

profile of v6, /device:TPU:121, one launch (start us, length us, event | category | flops | bytes accessed | tf_op | source)
XLA Modules:
  0.0 91.2 jit_solution(1818497064185589405)
XLA Ops:
  0.6 0.0 copy-start
  0.6 0.8 copy-done
  1.5 0.0 copy-start.1
  1.5 88.4 %shard_map.59 = (f32[1,32,512]{2,1,0:T(8,128)S(1)}, f32[1,32,1024]{2,1,0:T(8,128)S(1)}) custom-call(bf16[1,1024,512]{2,1,0:T(8,128)(2,1)} %maps_hbm.1, f32[1,32,512]{2,1,0:T(8,128)S(1)} %copy-done, bf16[1,512,2048]{2,1,0:T(8,128)(2,1)} %spikes_hbm.1), custom_call_target="tpu_custom_call" | custom-call | tf_op jit(solution)/shard_map/pallas_call | solution.py:604
  89.9 0.6 add.3
  90.5 0.0 copy-done.1
  90.5 0.7 sub.3
Async XLA Ops:
  0.6 0.8 copy-start
  1.5 89.1 %copy-start.1 = (f32[1,32,1024]{2,1,0:T(8,128)S(1)}, f32[1,32,1024]{2,1,0:T(8,128)}, u32[]{:S(2)}) copy-start(f32[1,32,1024]{2,1,0:T(8,128)} %param.7) | copy-start | bytes 393220

commit v7 on v6

--- a/solution.py
+++ b/solution.py
@@ -10,8 +10,8 @@
 MESH = pl.DeviceIdType.MESH
 RING = 4
 CHAIN_ROWS = 2
-HELPED_ROWS = 2
-PRODUCT_ROW = 6
+HELPED_ROWS = 4
+PRODUCT_ROW = 4
 
 
 def split_rows(value):
@@ -64,8 +64,10 @@
     ringed = row >= CHAIN_ROWS
     helped = jnp.logical_and(ringed, row < CHAIN_ROWS + HELPED_ROWS)
     alone = row >= CHAIN_ROWS + HELPED_ROWS
-    helper = jnp.logical_and(chained, row >= CHAIN_ROWS - HELPED_ROWS)
-    mirrored = (2 * CHAIN_ROWS - 1 - row) * RING
+    helping = rows_total - 4
+    served = CHAIN_ROWS + lax.rem(row - helping + 4 * rows_total - CHAIN_ROWS, 4)
+    helper = jnp.logical_and(row >= helping, served < CHAIN_ROWS + HELPED_ROWS)
+    mirrored = jnp.where(helped, helping + lax.rem(row, 4), served) * RING
     relayed = maps_hbm.shape[1] // 4
     last_chain = CHAIN_ROWS * RING - 1
     right, left = base + lax.rem(x + 1, RING), base + lax.rem(x + 3, RING)
@@ -95,10 +97,6 @@
         def _():
             greet(0, other)
 
-        @pl.when(helper)
-        def _():
-            greet(mirrored + x, tip)
-
     @pl.when(ringed)
     def _():
         for step in range(1, RING):
@@ -110,6 +108,10 @@
         @pl.when(row >= PRODUCT_ROW)
         def _():
             greet(before, other)
+
+        @pl.when(helper)
+        def _():
+            greet(mirrored + x, tip)
 
     own_map = pltpu.make_async_copy(maps_hbm.at[0], maps.at[x, tip], local_sem.at[0])
     own_map.start()
@@ -197,10 +199,6 @@
         def _():
             many_in[...] = jnp.zeros_like(many_in)
 
-        @pl.when(jnp.logical_and(helper, row == CHAIN_ROWS - 1))
-        def _():
-            pass_on()
-
         total = [None, None]
         for k in range(2):
             @pl.when(me > 0)
@@ -229,10 +227,6 @@
                     states.at[piece], few_in, home_send.at[piece, 0], wave_recv.at[2], last_chain + 1 + piece, tip
                 ).start()
 
-        @pl.when(jnp.logical_and(helper, row < CHAIN_ROWS - 1))
-        def _():
-            pass_on()
-
         to_sibling = remote(many_in, prior_many, side_send.at[1], side_recv.at[1], me, other)
         to_sibling.start()
         for h in range(2):
@@ -240,12 +234,6 @@
         to_sibling.wait_recv()
         for h in range(2):
             full[tip_rows, h * half : (h + 1) * half] = prior_many[h]
-
-        @pl.when(helper)
-        def _():
-            for k in range(2):
-                for step in range(1, RING):
-                    from_relay(step, k).wait_send()
 
         to_sibling.wait_send()
         tips_copy.wait_send()
@@ -390,6 +378,10 @@
             own_sibling_map(part).start()
         spikes_out.start()
 
+        @pl.when(helper)
+        def _():
+            pass_on()
+
         @pl.when(alone)
         def _():
             whole.middle()
@@ -547,6 +539,12 @@
         @pl.when(alone)
         def _():
             whole.drain()
+
+        @pl.when(helper)
+        def _():
+            for k in range(2):
+                for step in range(1, RING):
+                    from_relay(step, k).wait_send()
 
         @pl.when(helped)
         def _():

time: 91.7 us -> 104 us (1.13)
  Pallas kernels: 88.4 us -> 102 us
    pallas_call x1, Pallas kernels: 88.4 us -> 102 us  [on_device(): pl.pallas_call(functools.partial(sweep, rows_total), out_shape=(jax.Shape...]
where the time goes in v7:
time: 104 us
  Pallas kernels  102 us (98%)
  other arithmetic  1.31 us (1%)
    pallas_call x1, Pallas kernels, on_device(): pl.pallas_call(functools.partial(sweep, rows_total), out_shape=(jax.Shape...  102 us

profile of v7, /device:TPU:121, one launch (start us, length us, event | category | flops | bytes accessed | tf_op | source)
XLA Modules:
  0.0 104.3 jit_solution(5101279020688908576)
XLA Ops:
  0.6 0.0 copy-start
  0.6 0.8 copy-done
  1.5 0.0 copy-start.1
  1.5 101.5 %shard_map.59 = (f32[1,32,512]{2,1,0:T(8,128)S(1)}, f32[1,32,1024]{2,1,0:T(8,128)S(1)}) custom-call(bf16[1,1024,512]{2,1,0:T(8,128)(2,1)} %maps_hbm.1, f32[1,32,512]{2,1,0:T(8,128)S(1)} %copy-done, bf16[1,512,2048]{2,1,0:T(8,128)(2,1)} %spikes_hbm.1), custom_call_target="tpu_custom_call" | custom-call | tf_op jit(solution)/shard_map/pallas_call | solution.py:602
  103.0 0.6 add.3
  103.6 0.0 copy-done.1
  103.6 0.7 sub.3
Async XLA Ops:
  0.6 0.8 copy-start
  1.5 102.2 %copy-start.1 = (f32[1,32,1024]{2,1,0:T(8,128)S(1)}, f32[1,32,1024]{2,1,0:T(8,128)}, u32[]{:S(2)}) copy-start(f32[1,32,1024]{2,1,0:T(8,128)} %param.7) | copy-start | bytes 393220

commit v8 on v7

--- a/solution.py
+++ b/solution.py
@@ -353,7 +353,7 @@
                 to_relay(k).start()
             rest.start()
 
-        @pl.when(alone)
+        @pl.when(jnp.logical_and(alone, jnp.logical_not(helper)))
         def _():
             whole.start()
 
@@ -381,6 +381,10 @@
         @pl.when(helper)
         def _():
             pass_on()
+
+        @pl.when(jnp.logical_and(alone, helper))
+        def _():
+            whole.start()
 
         @pl.when(alone)
         def _():

time: 104 us -> 85.8 us (0.82)
  Pallas kernels: 102 us -> 82.5 us
    pallas_call x1, Pallas kernels: 102 us -> 82.5 us  [on_device(): pl.pallas_call(functools.partial(sweep, rows_total), out_shape=(jax.Shape...]
where the time goes in v8:
time: 85.8 us; the launch traced here: 85.3 us
  Pallas kernels  82.5 us (96%)
  other arithmetic  1.31 us (2%)
    pallas_call x1, Pallas kernels, on_device(): pl.pallas_call(functools.partial(sweep, rows_total), out_shape=(jax.Shape...  82.5 us

profile of v8, /device:TPU:121, one launch (start us, length us, event | category | flops | bytes accessed | tf_op | source)
XLA Modules:
  0.0 85.3 jit_solution(7080804054533188077)
XLA Ops:
  0.6 0.0 copy-start
  0.6 0.8 copy-done
  1.5 0.0 copy-start.1
  1.5 82.5 %shard_map.59 = (f32[1,32,512]{2,1,0:T(8,128)S(1)}, f32[1,32,1024]{2,1,0:T(8,128)S(1)}) custom-call(bf16[1,1024,512]{2,1,0:T(8,128)(2,1)} %maps_hbm.1, f32[1,32,512]{2,1,0:T(8,128)S(1)} %copy-done, bf16[1,512,2048]{2,1,0:T(8,128)(2,1)} %spikes_hbm.1), custom_call_target="tpu_custom_call" | custom-call | tf_op jit(solution)/shard_map/pallas_call | solution.py:606
  84.0 0.6 add.3
  84.6 0.0 copy-done.1
  84.6 0.7 sub.3
Async XLA Ops:
  0.6 0.8 copy-start
  1.5 83.1 %copy-start.1 = (f32[1,32,1024]{2,1,0:T(8,128)S(1)}, f32[1,32,1024]{2,1,0:T(8,128)}, u32[]{:S(2)}) copy-start(f32[1,32,1024]{2,1,0:T(8,128)} %param.7) | copy-start | bytes 393220

commit v9 on v8

--- a/solution.py
+++ b/solution.py
@@ -27,30 +27,33 @@
     return [piece[:rows] + piece[rows:] for piece in out]
 
 
-def four_maps(maps, tip, high, low):
+def leading_maps(last, maps, tip, high, low):
     half = maps.shape[3]
     block = min(256, half)
-    for turn, step in enumerate((2, 1, 0)):
+    for turn, step in enumerate(range(last - 1, -1, -1)):
         factor = jnp.concatenate([maps[step, 0], maps[step, 1]], 1)
         for start in range(0, half, block):
             columns = slice(start, start + block)
             if turn == 0:
-                total = jnp.dot(factor, maps[3, tip, :, columns], preferred_element_type=jnp.float32)
+                total = jnp.dot(factor, maps[last, tip, :, columns], preferred_element_type=jnp.float32)
             else:
                 total = jnp.dot(factor, high[(turn - 1) % 2, :, columns], preferred_element_type=jnp.float32)
                 total += jnp.dot(factor, low[(turn - 1) % 2, :, columns], preferred_element_type=jnp.float32)
             top = total.astype(jnp.bfloat16)
             high[turn % 2, :, columns] = top
             low[turn % 2, :, columns] = (total - top.astype(jnp.float32)).astype(jnp.bfloat16)
+    return (last - 1) % 2
 
 
 def sweep(
     rows_total, maps_hbm, tips_hbm, spikes_hbm, interface_ref, product_ref,
     maps, tips_ref, tips_out, tips_both, tips_few, tips_many, few_in, pair_in, columns_in, columns_out, local,
     high, low, many_in, many_out, states, prior, prior_many, full, spikes,
-    local_sem, sib_send, sib_recv, quarter_send, quarter_recv, relay, relay_send, relay_recv, relay_sib_send, relay_sib_recv,
+    local_sem, sib_send, sib_recv, quarter_send, quarter_recv, relay, relay_open, relay_send, relay_recv,
+    relay_sib_send, relay_sib_recv,
     link_send, link_recv, fwd_send, opp_recv,
     tip_send, tip_recv, wave_send, wave_recv, home_send, home_recv, side_send, side_recv,
+    last_in, last_send, last_recv,
 ):
     me, tip = lax.axis_index("dom"), lax.axis_index("tip")
     x, row = lax.rem(me, RING), lax.div(me, RING)
@@ -109,7 +112,7 @@
         def _():
             greet(before, other)
 
-        @pl.when(helper)
+        @pl.when(helped)
         def _():
             greet(mirrored + x, tip)
 
@@ -128,7 +131,11 @@
     @pl.when(ringed)
     def _():
         after = jnp.where(row == rows_total - 1, 0, jnp.where(row >= PRODUCT_ROW - 1, 2, 1))
-        pl.semaphore_wait(barrier, 2 * RING - 1 + after + jnp.where(helped, 1, 0))
+        pl.semaphore_wait(barrier, 2 * RING - 1 + after + jnp.where(helper, 1, 0))
+
+        @pl.when(helper)
+        def _():
+            pl.semaphore_signal(relay_open, inc=1, device_id=(mirrored + x, tip), device_id_type=MESH)
 
     pieces = [slice(0, cut), slice(cut, depth)]
 
@@ -349,8 +356,6 @@
 
         @pl.when(helped)
         def _():
-            for k in range(2):
-                to_relay(k).start()
             rest.start()
 
         @pl.when(jnp.logical_and(alone, jnp.logical_not(helper)))
@@ -377,6 +382,12 @@
         for part in range(2):
             own_sibling_map(part).start()
         spikes_out.start()
+
+        @pl.when(helped)
+        def _():
+            pl.semaphore_wait(relay_open, 1)
+            for k in range(2):
+                to_relay(k).start()
 
         @pl.when(helper)
         def _():
@@ -444,6 +455,11 @@
                 tips_few[step, h] = own_of(tips_both[step, h])
 
         final_row = row == rows_total - 1
+        to_the_end = jnp.logical_and(final_row, x == RING - 1)
+
+        def to_last(to):
+            dom = base + RING - 1
+            return remote(columns_out, last_in.at[x, tip], last_send.at[to], last_recv.at[x, tip], dom, to)
         direct = row < PRODUCT_ROW
 
         def onward_rows(to):
@@ -478,16 +494,30 @@
 
         @pl.when(jnp.logical_not(direct))
         def _():
-            @pl.when(jnp.logical_not(final_row))
-            def _():
-                four_maps(maps, tip, high, low)
+            def prepare(last):
+                leading_maps(last, maps, tip, high, low)
                 state = jnp.concatenate([tips_both[0, 0], tips_both[0, 1]], 1)
-                for step in (1, 2):
+                for step in range(1, last):
                     fresh = times_map(state, maps[step, 0], maps[step, 1])
                     state = jnp.concatenate([fresh[h] + tips_both[step, h] for h in range(2)], 1)
                 parts = split_rows(state)
-                fresh = jnp.dot(parts, maps[3, tip], preferred_element_type=jnp.float32)
-                local[...] = fresh[: 2 * few] + fresh[2 * few :] + tips_both[3, tip]
+                fresh = jnp.dot(parts, maps[last, tip], preferred_element_type=jnp.float32)
+                local[...] = fresh[: 2 * few] + fresh[2 * few :] + tips_both[last, tip]
+
+            def product_step(last):
+                slot = (last - 1) % 2
+                parts = split_rows(jnp.concatenate([columns_in[0], columns_in[1]], 1))
+                fresh = jnp.dot(parts, high[slot], preferred_element_type=jnp.float32)
+                fresh = fresh + jnp.dot(parts, low[slot], preferred_element_type=jnp.float32)
+                columns_out[...] = fresh[: 2 * few] + fresh[2 * few :] + local[...]
+
+            @pl.when(jnp.logical_not(final_row))
+            def _():
+                prepare(RING - 1)
+
+            @pl.when(final_row)
+            def _():
+                prepare(RING - 2)
 
             @pl.when(row == PRODUCT_ROW)
             def _():
@@ -504,41 +534,68 @@
                     columns_in.at[core], columns_in.at[core], wave_send.at[0], wave_recv.at[5 + core], me, other
                 ).wait_recv()
 
-            @pl.when(final_row)
+            @pl.when(row > PRODUCT_ROW)
             def _():
                 for core in range(2):
                     columns_arrive(core)
 
             @pl.when(jnp.logical_not(final_row))
             def _():
-                @pl.when(row > PRODUCT_ROW)
-                def _():
-                    for core in range(2):
-                        columns_arrive(core)
-
-                parts = split_rows(jnp.concatenate([columns_in[0], columns_in[1]], 1))
-                fresh = jnp.dot(parts, high[0], preferred_element_type=jnp.float32)
-                fresh = fresh + jnp.dot(parts, low[0], preferred_element_type=jnp.float32)
-                columns_out[...] = fresh[: 2 * few] + fresh[2 * few :] + local[...]
+                product_step(RING - 1)
                 for to in range(2):
                     onward_columns(to).start()
+
+            @pl.when(final_row)
+            def _():
+                product_step(RING - 2)
+                for to in range(2):
+                    @pl.when(jnp.logical_or(x != RING - 1, tip != to))
+                    def _():
+                        to_last(to).start()
+
+                @pl.when(x == RING - 1)
+                def _():
+                    last_in[x, tip] = columns_out[...]
 
             for h in range(2):
                 few_in[:, h * half : (h + 1) * half] = own_of(columns_in[h])
             send_home(0)
             state = few_in[...]
-            for step in range(RING - 1):
+            for step in range(RING - 2):
                 state = next_state(step, state)
                 send_home(step + 1)
 
-        for piece in range(2 * RING):
-            @pl.when(piece != mine)
-            def _():
-                remote(
-                    prior.at[piece], prior.at[piece], home_send.at[0, 0], home_recv.at[piece], me, other
-                ).wait_recv()
-        for piece in range(2 * RING):
-            full[piece * few : (piece + 1) * few, :] = prior[piece]
+            @pl.when(jnp.logical_not(final_row))
+            def _():
+                next_state(RING - 2, state)
+                send_home(RING - 1)
+
+        @pl.when(to_the_end)
+        def _():
+            for chip in range(RING):
+                for core in range(2):
+                    @pl.when(jnp.logical_or(chip != x, core != tip))
+                    def _():
+                        block = last_in.at[chip, core]
+                        remote(block, block, last_send.at[0], last_recv.at[chip, core], me, other).wait_recv()
+            for chip in range(RING):
+                for core in range(2):
+                    columns = slice(core * half, (core + 1) * half)
+                    for group in range(2):
+                        start = group * many + chip * few
+                        block = last_in[chip, core, group * few : (group + 1) * few, :]
+                        full[start : start + few, columns] = block
+
+        @pl.when(jnp.logical_not(to_the_end))
+        def _():
+            for piece in range(2 * RING):
+                @pl.when(piece != mine)
+                def _():
+                    remote(
+                        prior.at[piece], prior.at[piece], home_send.at[0, 0], home_recv.at[piece], me, other
+                    ).wait_recv()
+            for piece in range(2 * RING):
+                full[piece * few : (piece + 1) * few, :] = prior[piece]
 
         @pl.when(alone)
         def _():
@@ -577,11 +634,22 @@
             for to in range(2):
                 onward_columns(to).wait_send()
 
-        for step in range(RING):
+        for step in range(RING - 1):
             for to in range(2):
                 @pl.when(jnp.logical_or(x != step, tip != to))
                 def _():
                     home_copy(step, to).wait_send()
+
+        for to in range(2):
+            @pl.when(jnp.logical_or(x != RING - 1, tip != to))
+            def _():
+                @pl.when(final_row)
+                def _():
+                    to_last(to).wait_send()
+
+                @pl.when(jnp.logical_not(final_row))
+                def _():
+                    home_copy(RING - 1, to).wait_send()
 
     own_spikes.wait()
     spikes_out.wait()
@@ -642,6 +710,7 @@
             dma((2, 2)),
             dma((2, 2)),
             pltpu.VMEM((2, depth // 8, half), b16),
+            pltpu.SemaphoreType.REGULAR,
             dma((RING, 2)),
             dma((RING, 2)),
             dma((RING, 2)),
@@ -658,6 +727,9 @@
             dma((2 * RING,)),
             dma((2,)),
             dma((2,)),
+            pltpu.VMEM((RING, 2, 2 * few, half), f32),
+            dma((2,)),
+            dma((RING, 2)),
         ],
         compiler_params=pltpu.CompilerParams(
             collective_id=0, has_side_effects=True, vmem_limit_bytes=53 << 20

time: 85.8 us -> 86.1 us (level)
  no operation moved by 1% of the time
where the time goes in v9:
time: 86.1 us; the launch traced here: 86 us
  Pallas kernels  83.2 us (97%)
  other arithmetic  1.31 us (2%)
    pallas_call x1, Pallas kernels, on_device(): pl.pallas_call(functools.partial(sweep, rows_total), out_shape=(jax.Shape...  83.2 us

profile of v9, /device:TPU:121, one launch (start us, length us, event | category | flops | bytes accessed | tf_op | source)
XLA Modules:
  0.0 86.0 jit_solution(14314862289466316297)
XLA Ops:
  0.6 0.0 copy-start
  0.6 0.8 copy-done
  1.5 0.0 copy-start.1
  1.5 83.2 %shard_map.59 = (f32[1,32,512]{2,1,0:T(8,128)S(1)}, f32[1,32,1024]{2,1,0:T(8,128)S(1)}) custom-call(bf16[1,1024,512]{2,1,0:T(8,128)(2,1)} %maps_hbm.1, f32[1,32,512]{2,1,0:T(8,128)S(1)} %copy-done, bf16[1,512,2048]{2,1,0:T(8,128)(2,1)} %spikes_hbm.1), custom_call_target="tpu_custom_call" | custom-call | tf_op jit(solution)/shard_map/pallas_call | solution.py:674
  84.7 0.6 add.3
  85.3 0.0 copy-done.1
  85.3 0.7 sub.3
Async XLA Ops:
  0.6 0.8 copy-start
  1.5 83.8 %copy-start.1 = (f32[1,32,1024]{2,1,0:T(8,128)S(1)}, f32[1,32,1024]{2,1,0:T(8,128)}, u32[]{:S(2)}) copy-start(f32[1,32,1024]{2,1,0:T(8,128)} %param.7) | copy-start | bytes 393220

commit v10 on v9

--- a/solution.py
+++ b/solution.py
@@ -10,7 +10,14 @@
 MESH = pl.DeviceIdType.MESH
 RING = 4
 CHAIN_ROWS = 2
-HELPED_ROWS = 4
+HELPERS = {
+    2: ((14, 3), (1, 2)),
+    3: ((15, 4),),
+    4: ((13, 4),),
+    5: ((12, 3),),
+    6: ((10, 2),),
+    7: ((11, 2),),
+}
 PRODUCT_ROW = 4
 
 
@@ -65,13 +72,36 @@
     width = spikes_hbm.shape[2] // 2
     chained = row < CHAIN_ROWS
     ringed = row >= CHAIN_ROWS
-    helped = jnp.logical_and(ringed, row < CHAIN_ROWS + HELPED_ROWS)
-    alone = row >= CHAIN_ROWS + HELPED_ROWS
-    helping = rows_total - 4
-    served = CHAIN_ROWS + lax.rem(row - helping + 4 * rows_total - CHAIN_ROWS, 4)
-    helper = jnp.logical_and(row >= helping, served < CHAIN_ROWS + HELPED_ROWS)
-    mirrored = jnp.where(helped, helping + lax.rem(row, 4), served) * RING
-    relayed = maps_hbm.shape[1] // 4
+    def among(rows):
+        return functools.reduce(jnp.logical_or, [row == r for r in rows])
+
+    def first_chip(pairs):
+        value = pairs[0][1]
+        for this, that in pairs[1:]:
+            value = jnp.where(row == this, that, value)
+        return value * RING
+
+    by_shares, by_part = {}, {}
+    for r, helpers in HELPERS.items():
+        by_shares.setdefault(tuple(n for _, n in helpers), []).append(r)
+        first = 0
+        for which, (h, n) in enumerate(helpers):
+            by_part.setdefault((first, n, which, h < CHAIN_ROWS), []).append((h, r))
+            first += n
+    helped = []
+    for shares, rows in by_shares.items():
+        parts = [
+            (sum(shares[:which]), shares[which], first_chip([(r, HELPERS[r][which][0]) for r in rows]))
+            for which in range(len(shares))
+        ]
+        helped.append((among(rows), sum(shares), parts))
+    helping = [
+        (among([h for h, _ in pairs]), first, n, which, first_chip(pairs), in_chain)
+        for (first, n, which, in_chain), pairs in by_part.items()
+    ]
+    all_helped = among(list(HELPERS))
+    all_helping = among([h for helpers in HELPERS.values() for h, _ in helpers])
+    unit = maps_hbm.shape[1] // 16
     last_chain = CHAIN_ROWS * RING - 1
     right, left = base + lax.rem(x + 1, RING), base + lax.rem(x + 3, RING)
     opposite = base + lax.rem(x + 2, RING)
@@ -112,9 +142,11 @@
         def _():
             greet(before, other)
 
-        @pl.when(helped)
-        def _():
-            greet(mirrored + x, tip)
+        for those, _, parts in helped:
+            @pl.when(those)
+            def _():
+                for _, _, chip in parts:
+                    greet(chip + x, tip)
 
     own_map = pltpu.make_async_copy(maps_hbm.at[0], maps.at[x, tip], local_sem.at[0])
     own_map.start()
@@ -124,18 +156,21 @@
     own_spikes.start()
     own_tips = pltpu.make_async_copy(tips_hbm.at[0], tips_ref, local_sem.at[2])
     own_tips.start()
+    asked = jnp.where(all_helping, 1, 0)
+
     @pl.when(chained)
     def _():
-        pl.semaphore_wait(barrier, jnp.where(me == last_chain, 1 + RING, jnp.where(me == 0, 3, 2)))
+        pl.semaphore_wait(barrier, jnp.where(me == last_chain, 1 + RING, jnp.where(me == 0, 3, 2)) + asked)
 
     @pl.when(ringed)
     def _():
         after = jnp.where(row == rows_total - 1, 0, jnp.where(row >= PRODUCT_ROW - 1, 2, 1))
-        pl.semaphore_wait(barrier, 2 * RING - 1 + after + jnp.where(helper, 1, 0))
-
-        @pl.when(helper)
-        def _():
-            pl.semaphore_signal(relay_open, inc=1, device_id=(mirrored + x, tip), device_id_type=MESH)
+        pl.semaphore_wait(barrier, 2 * RING - 1 + after + asked)
+
+    for those, _, _, which, chip, _ in helping:
+        @pl.when(those)
+        def _():
+            pl.semaphore_signal(relay_open.at[which], inc=1, device_id=(chip + x, tip), device_id_type=MESH)
 
     pieces = [slice(0, cut), slice(cut, depth)]
 
@@ -157,23 +192,27 @@
         return remote(tips_hbm.at[0, rows, :], many_in.at[tip], wave_send.at[to], wave_recv.at[tip], 1, to)
 
     def relay_rows(k):
-        start = depth - relayed + k * (relayed // 2)
-        return slice(start, start + relayed // 2)
-
-    def to_relay(k):
+        return slice(depth - (k + 1) * unit, depth - k * unit)
+
+    def to_relay(k, chip):
         src = maps_hbm.at[0, relay_rows(k)]
-        return remote(src, relay.at[k], relay_send.at[0, k], relay_recv.at[0, k], mirrored + x, tip)
-
-    def from_relay(step, k):
+        return remote(src, relay.at[k], relay_send.at[0, k], relay_recv.at[0, k], chip + x, tip)
+
+    def from_relay(step, k, chip):
         dst = maps.at[x, tip, relay_rows(k)]
-        dom = mirrored + lax.rem(x + step, RING)
+        dom = chip + lax.rem(x + step, RING)
         return remote(relay.at[k], dst, relay_send.at[step, k], relay_recv.at[step, k], dom, tip)
 
-    def pass_on():
-        for k in range(2):
+    def pass_on(first, n, chip):
+        for k in range(first, first + n):
             remote(relay.at[k], relay.at[k], relay_send.at[0, k], relay_recv.at[0, k], me, other).wait_recv()
             for step in range(1, RING):
-                from_relay(step, k).start()
+                from_relay(step, k, chip).start()
+
+    def relay_drain(first, n, chip):
+        for k in range(first, first + n):
+            for step in range(1, RING):
+                from_relay(step, k, chip).wait_send()
 
     @pl.when(chained)
     def _():
@@ -206,6 +245,12 @@
         def _():
             many_in[...] = jnp.zeros_like(many_in)
 
+        for those, first, n, _, chip, in_chain in helping:
+            if in_chain:
+                @pl.when(those)
+                def _():
+                    pass_on(first, n, chip)
+
         total = [None, None]
         for k in range(2):
             @pl.when(me > 0)
@@ -242,6 +287,12 @@
         for h in range(2):
             full[tip_rows, h * half : (h + 1) * half] = prior_many[h]
 
+        for those, first, n, _, chip, in_chain in helping:
+            if in_chain:
+                @pl.when(those)
+                def _():
+                    relay_drain(first, n, chip)
+
         to_sibling.wait_send()
         tips_copy.wait_send()
         for part in range(2):
@@ -312,9 +363,10 @@
                 block = maps.at[lax.rem(x + 2, RING), other, self.rows(side, k)]
                 remote(block, block, quarter_send.at[side, k], quarter_recv.at[side, k], me, other).wait_recv()
 
-            def start(self):
-                for part, side in ((0, 0), (1, 1), (1, 0), (0, 1)):
-                    self.own(part, side).start()
+            def start(self, which=(0, 1)):
+                for turn in which:
+                    for part, side in (((0, 0), (1, 1)), ((1, 0), (0, 1)))[turn]:
+                        self.own(part, side).start()
 
             def middle(self):
                 for part, side in ((0, 0), (1, 1)):
@@ -348,19 +400,27 @@
                     for step in (1, 3):
                         self.to_sibling(step, part).wait_send()
 
-        whole, rest = Gather(depth), Gather(depth - relayed)
+        whole = Gather(depth)
+        gathers = [Gather(depth - count * unit) for _, count, _ in helped]
 
         def relayed_to_sibling(step, k):
             block = maps.at[lax.rem(x + RING - step, RING), tip, relay_rows(k)]
             return remote(block, block, relay_sib_send.at[step, k], relay_sib_recv.at[step, k], me, other)
 
-        @pl.when(helped)
-        def _():
-            rest.start()
-
-        @pl.when(jnp.logical_and(alone, jnp.logical_not(helper)))
+        for (those, _, _), gather in zip(helped, gathers):
+            @pl.when(those)
+            def _():
+                gather.start()
+
+        @pl.when(jnp.logical_not(jnp.logical_or(all_helped, all_helping)))
         def _():
             whole.start()
+
+        for those, _, n, _, _, in_chain in helping:
+            if not in_chain and n < 3:
+                @pl.when(those)
+                def _():
+                    whole.start((0,))
 
         own_tips.wait()
         for piece in range(RING):
@@ -383,38 +443,42 @@
             own_sibling_map(part).start()
         spikes_out.start()
 
-        @pl.when(helped)
-        def _():
-            pl.semaphore_wait(relay_open, 1)
-            for k in range(2):
-                to_relay(k).start()
-
-        @pl.when(helper)
-        def _():
-            pass_on()
-
-        @pl.when(jnp.logical_and(alone, helper))
-        def _():
-            whole.start()
-
-        @pl.when(alone)
+        for those, _, parts in helped:
+            @pl.when(those)
+            def _():
+                for which, (first, n, chip) in reversed(list(enumerate(parts))):
+                    pl.semaphore_wait(relay_open.at[which], 1)
+                    for k in range(first, first + n):
+                        to_relay(k, chip).start()
+
+        for those, first, n, _, chip, in_chain in helping:
+            if not in_chain:
+                @pl.when(those)
+                def _():
+                    pass_on(first, n, chip)
+                    whole.start((1,) if n < 3 else (0, 1))
+
+        @pl.when(jnp.logical_not(all_helped))
         def _():
             whole.middle()
             whole.last()
 
-        @pl.when(helped)
-        def _():
-            rest.middle()
-            for k in range(2):
-                for step in range(1, RING):
-                    block = maps.at[lax.rem(x + RING - step, RING), tip, relay_rows(k)]
-                    remote(block, block, relay_send.at[step, k], relay_recv.at[step, k], me, other).wait_recv()
-                    relayed_to_sibling(step, k).start()
-            rest.last()
-            for k in range(2):
-                for step in range(1, RING):
-                    block = maps.at[lax.rem(x + RING - step, RING), other, relay_rows(k)]
-                    remote(block, block, relay_sib_send.at[step, k], relay_sib_recv.at[step, k], me, other).wait_recv()
+        for (those, count, _), gather in zip(helped, gathers):
+            @pl.when(those)
+            def _():
+                gather.middle()
+                for k in range(count):
+                    for step in range(1, RING):
+                        block = maps.at[lax.rem(x + RING - step, RING), tip, relay_rows(k)]
+                        remote(block, block, relay_send.at[step, k], relay_recv.at[step, k], me, other).wait_recv()
+                        relayed_to_sibling(step, k).start()
+                gather.last()
+                for k in range(count):
+                    for step in range(1, RING):
+                        block = maps.at[lax.rem(x + RING - step, RING), other, relay_rows(k)]
+                        remote(
+                            block, block, relay_sib_send.at[step, k], relay_sib_recv.at[step, k], me, other
+                        ).wait_recv()
 
         own_map.wait()
         for part in range(2):
@@ -504,6 +568,11 @@
                 fresh = jnp.dot(parts, maps[last, tip], preferred_element_type=jnp.float32)
                 local[...] = fresh[: 2 * few] + fresh[2 * few :] + tips_both[last, tip]
 
+            def start_state():
+                for h in range(2):
+                    few_in[:, h * half : (h + 1) * half] = own_of(columns_in[h])
+                send_home(0)
+
             def product_step(last):
                 slot = (last - 1) % 2
                 parts = split_rows(jnp.concatenate([columns_in[0], columns_in[1]], 1))
@@ -547,6 +616,7 @@
 
             @pl.when(final_row)
             def _():
+                start_state()
                 product_step(RING - 2)
                 for to in range(2):
                     @pl.when(jnp.logical_or(x != RING - 1, tip != to))
@@ -557,9 +627,10 @@
                 def _():
                     last_in[x, tip] = columns_out[...]
 
-            for h in range(2):
-                few_in[:, h * half : (h + 1) * half] = own_of(columns_in[h])
-            send_home(0)
+            @pl.when(jnp.logical_not(final_row))
+            def _():
+                start_state()
+
             state = few_in[...]
             for step in range(RING - 2):
                 state = next_state(step, state)
@@ -597,23 +668,25 @@
             for piece in range(2 * RING):
                 full[piece * few : (piece + 1) * few, :] = prior[piece]
 
-        @pl.when(alone)
+        @pl.when(jnp.logical_not(all_helped))
         def _():
             whole.drain()
 
-        @pl.when(helper)
-        def _():
-            for k in range(2):
-                for step in range(1, RING):
-                    from_relay(step, k).wait_send()
-
-        @pl.when(helped)
-        def _():
-            rest.drain()
-            for k in range(2):
-                to_relay(k).wait_send()
-                for step in range(1, RING):
-                    relayed_to_sibling(step, k).wait_send()
+        for those, first, n, _, chip, in_chain in helping:
+            if not in_chain:
+                @pl.when(those)
+                def _():
+                    relay_drain(first, n, chip)
+
+        for (those, _, parts), gather in zip(helped, gathers):
+            @pl.when(those)
+            def _():
+                gather.drain()
+                for first, n, chip in parts:
+                    for k in range(first, first + n):
+                        to_relay(k, chip).wait_send()
+                        for step in range(1, RING):
+                            relayed_to_sibling(step, k).wait_send()
 
         for part in range(2):
             own_sibling_map(part).wait_send()
@@ -709,12 +782,12 @@
             dma((RING, 2)),
             dma((2, 2)),
             dma((2, 2)),
-            pltpu.VMEM((2, depth // 8, half), b16),
-            pltpu.SemaphoreType.REGULAR,
-            dma((RING, 2)),
-            dma((RING, 2)),
-            dma((RING, 2)),
-            dma((RING, 2)),
+            pltpu.VMEM((5, depth // 16, half), b16),
+            pltpu.SemaphoreType.REGULAR((2,)),
+            dma((RING, 5)),
+            dma((RING, 5)),
+            dma((RING, 5)),
+            dma((RING, 5)),
             dma((2, 2)),
             dma((2, 2)),
             dma((2, 2)),

time: 86.1 us -> 83.5 us (0.970)
  Pallas kernels: 83.2 us -> 80.6 us
    pallas_call x1, Pallas kernels: 83.2 us -> 80.6 us  [on_device(): pl.pallas_call(functools.partial(sweep, rows_total), out_shape=(jax.Shape...]
where the time goes in v10:
time: 83.5 us; the launch traced here: 83.4 us
  Pallas kernels  80.6 us (97%)
  other arithmetic  1.31 us (2%)
  local copies, waits for them, and re-layouts  0.84 us (1%)
    pallas_call x1, Pallas kernels, on_device(): pl.pallas_call(functools.partial(sweep, rows_total), out_shape=(jax.Shape...  80.6 us

profile of v10, /device:TPU:121, one launch (start us, length us, event | category | flops | bytes accessed | tf_op | source)
XLA Modules:
  0.0 83.4 jit_solution(18420864234297564883)
XLA Ops:
  0.6 0.0 copy-start
  0.6 0.8 copy-done
  1.5 0.0 copy-start.1
  1.5 80.6 %shard_map.59 = (f32[1,32,512]{2,1,0:T(8,128)S(1)}, f32[1,32,1024]{2,1,0:T(8,128)S(1)}) custom-call(bf16[1,1024,512]{2,1,0:T(8,128)(2,1)} %maps_hbm.1, f32[1,32,512]{2,1,0:T(8,128)S(1)} %copy-done, bf16[1,512,2048]{2,1,0:T(8,128)(2,1)} %spikes_hbm.1), custom_call_target="tpu_custom_call" | custom-call | tf_op jit(solution)/shard_map/pallas_call | solution.py:747
  82.0 0.6 add.3
  82.7 0.0 copy-done.1
  82.7 0.7 sub.3
Async XLA Ops:
  0.6 0.8 %copy-start = (f32[1,32,512]{2,1,0:T(8,128)S(1)}, f32[1,32,512]{2,1,0:T(8,128)}, u32[]{:S(2)}) copy-start(f32[1,32,512]{2,1,0:T(8,128)} %tips_hbm.1) | copy-start | bytes 196612
  1.5 81.2 %copy-start.1 = (f32[1,32,1024]{2,1,0:T(8,128)S(1)}, f32[1,32,1024]{2,1,0:T(8,128)}, u32[]{:S(2)}) copy-start(f32[1,32,1024]{2,1,0:T(8,128)} %param.7) | copy-start | bytes 393220

commit v11 on v10

--- a/solution.py
+++ b/solution.py
@@ -807,7 +807,7 @@
         compiler_params=pltpu.CompilerParams(
             collective_id=0, has_side_effects=True, vmem_limit_bytes=53 << 20
         ),
-    )(band_maps, right_tips, spikes)
+    )(band_maps, pltpu.with_memory_space_constraint(right_tips, pltpu.HBM), spikes)
     return right_tips + interface, local_parts - product
 
 

time: 83.5 us -> 82.7 us (level)
  no operation moved by 1% of the time
where the time goes in v11:
time: 82.7 us; the launch traced here: 82.6 us
  Pallas kernels  80.6 us (97%)
  other arithmetic  1.31 us (2%)
    pallas_call x1, Pallas kernels, on_device(): pl.pallas_call(functools.partial(sweep, rows_total), out_shape=(jax.Shape...  80.6 us

profile of v11, /device:TPU:121, one launch (start us, length us, event | category | flops | bytes accessed | tf_op | source)
XLA Modules:
  0.0 82.6 jit_solution(13426462249566753333)
XLA Ops:
  0.6 0.0 copy-start
  0.6 0.0 copy-start.1
  0.7 80.6 %shard_map.59 = (f32[1,32,512]{2,1,0:T(8,128)S(1)}, f32[1,32,1024]{2,1,0:T(8,128)S(1)}) custom-call(bf16[1,1024,512]{2,1,0:T(8,128)(2,1)} %maps_hbm.1, f32[1,32,512]{2,1,0:T(8,128)} %tips_hbm.1, bf16[1,512,2048]{2,1,0:T(8,128)(2,1)} %spikes_hbm.1), custom_call_target="tpu_custom_call" | custom-call | tf_op jit(solution)/shard_map/pallas_call | solution.py:747
  81.3 0.0 copy-done
  81.3 0.6 add.3
  81.9 0.0 copy-done.1
  81.9 0.7 sub.3
Async XLA Ops:
  0.6 80.7 %copy-start = (f32[1,32,512]{2,1,0:T(8,128)S(1)}, f32[1,32,512]{2,1,0:T(8,128)}, u32[]{:S(2)}) copy-start(f32[1,32,512]{2,1,0:T(8,128)} %tips_hbm.1) | copy-start | bytes 196612
  0.6 81.3 %copy-start.1 = (f32[1,32,1024]{2,1,0:T(8,128)S(1)}, f32[1,32,1024]{2,1,0:T(8,128)}, u32[]{:S(2)}) copy-start(f32[1,32,1024]{2,1,0:T(8,128)} %param.7) | copy-start | bytes 393220

commit v12 on v11

--- a/solution.py
+++ b/solution.py
@@ -34,11 +34,14 @@
     return [piece[:rows] + piece[rows:] for piece in out]
 
 
-def leading_maps(last, maps, tip, high, low):
-    half = maps.shape[3]
+def leading_maps(last, maps, tips, tip, high, low, local):
+    depth, half = maps.shape[2], maps.shape[3]
+    count = local.shape[0]
+    local[...] = tips[last, tip]
     block = min(256, half)
     for turn, step in enumerate(range(last - 1, -1, -1)):
-        factor = jnp.concatenate([maps[step, 0], maps[step, 1]], 1)
+        rows = split_rows(jnp.concatenate([tips[step, 0], tips[step, 1]], 1))
+        factor = jnp.concatenate([jnp.concatenate([maps[step, 0], maps[step, 1]], 1), rows], 0)
         for start in range(0, half, block):
             columns = slice(start, start + block)
             if turn == 0:
@@ -46,10 +49,11 @@
             else:
                 total = jnp.dot(factor, high[(turn - 1) % 2, :, columns], preferred_element_type=jnp.float32)
                 total += jnp.dot(factor, low[(turn - 1) % 2, :, columns], preferred_element_type=jnp.float32)
+            local[:, columns] += total[depth : depth + count] + total[depth + count :]
+            total = total[:depth]
             top = total.astype(jnp.bfloat16)
             high[turn % 2, :, columns] = top
             low[turn % 2, :, columns] = (total - top.astype(jnp.float32)).astype(jnp.bfloat16)
-    return (last - 1) % 2
 
 
 def sweep(
@@ -230,9 +234,6 @@
         )
         tips_copy.start()
         spikes_out.start()
-        own_map.wait()
-        for part in range(2):
-            sibling_map_arrives(0, part)
         tips_copy.wait_recv()
 
         def many_send(h, dom):
@@ -257,6 +258,9 @@
             def _():
                 remote(many_in.at[k], many_in.at[k], wave_send.at[k], wave_recv.at[k], me, other).wait_recv()
 
+            if k == 0:
+                own_map.wait()
+            sibling_map_arrives(0, k)
             parts = split_rows(many_in[k])
             for h in range(2):
                 term = jnp.dot(parts, maps[x, h, k * half : (k + 1) * half, :], preferred_element_type=jnp.float32)
@@ -439,9 +443,6 @@
         for number, (step, to) in enumerate(partners):
             tip_copy(step, to, number).start()
         tips_both[x, tip] = tips_out[x]
-        for part in range(2):
-            own_sibling_map(part).start()
-        spikes_out.start()
 
         for those, _, parts in helped:
             @pl.when(those)
@@ -457,6 +458,10 @@
                 def _():
                     pass_on(first, n, chip)
                     whole.start((1,) if n < 3 else (0, 1))
+
+        for part in range(2):
+            own_sibling_map(part).start()
+        spikes_out.start()
 
         @pl.when(jnp.logical_not(all_helped))
         def _():
@@ -559,14 +564,7 @@
         @pl.when(jnp.logical_not(direct))
         def _():
             def prepare(last):
-                leading_maps(last, maps, tip, high, low)
-                state = jnp.concatenate([tips_both[0, 0], tips_both[0, 1]], 1)
-                for step in range(1, last):
-                    fresh = times_map(state, maps[step, 0], maps[step, 1])
-                    state = jnp.concatenate([fresh[h] + tips_both[step, h] for h in range(2)], 1)
-                parts = split_rows(state)
-                fresh = jnp.dot(parts, maps[last, tip], preferred_element_type=jnp.float32)
-                local[...] = fresh[: 2 * few] + fresh[2 * few :] + tips_both[last, tip]
+                leading_maps(last, maps, tips_both, tip, high, low, local)
 
             def start_state():
                 for h in range(2):

time: 82.7 us -> 82.5 us (level)
  no operation moved by 1% of the time
where the time goes in v12:
time: 82.5 us; the launch traced here: 82.3 us
  Pallas kernels  80.4 us (97%)
  other arithmetic  1.31 us (2%)
    pallas_call x1, Pallas kernels, on_device(): pl.pallas_call(functools.partial(sweep, rows_total), out_shape=(jax.Shape...  80.4 us

profile of v12, /device:TPU:121, one launch (start us, length us, event | category | flops | bytes accessed | tf_op | source)
XLA Modules:
  0.0 82.3 jit_solution(16012252228116057343)
XLA Ops:
  0.6 0.0 copy-start
  0.6 0.0 copy-start.1
  0.7 80.4 %shard_map.59 = (f32[1,32,512]{2,1,0:T(8,128)S(1)}, f32[1,32,1024]{2,1,0:T(8,128)S(1)}) custom-call(bf16[1,1024,512]{2,1,0:T(8,128)(2,1)} %maps_hbm.1, f32[1,32,512]{2,1,0:T(8,128)} %tips_hbm.1, bf16[1,512,2048]{2,1,0:T(8,128)(2,1)} %spikes_hbm.1), custom_call_target="tpu_custom_call" | custom-call | tf_op jit(solution)/shard_map/pallas_call | solution.py:745
  81.0 0.0 copy-done
  81.0 0.6 add.3
  81.7 0.0 copy-done.1
  81.7 0.7 sub.3
Async XLA Ops:
  0.6 80.4 %copy-start = (f32[1,32,512]{2,1,0:T(8,128)S(1)}, f32[1,32,512]{2,1,0:T(8,128)}, u32[]{:S(2)}) copy-start(f32[1,32,512]{2,1,0:T(8,128)} %tips_hbm.1) | copy-start | bytes 196612
  0.6 81.0 %copy-start.1 = (f32[1,32,1024]{2,1,0:T(8,128)S(1)}, f32[1,32,1024]{2,1,0:T(8,128)}, u32[]{:S(2)}) copy-start(f32[1,32,1024]{2,1,0:T(8,128)} %param.7) | copy-start | bytes 393220

commit v13 on v12

--- a/solution.py
+++ b/solution.py
@@ -501,7 +501,7 @@
             return remote(src, prior.at[mine], home_send.at[step, to], home_recv.at[mine], base + step, to)
 
         def send_home(step):
-            for to in range(2):
+            for to in (tip, other):
                 @pl.when(jnp.logical_or(x != step, tip != to))
                 def _():
                     home_copy(step, to).start()
@@ -555,7 +555,7 @@
 
             @pl.when(jnp.logical_and(row == PRODUCT_ROW - 1, jnp.logical_not(final_row)))
             def _():
-                for to in range(2):
+                for to in (tip, other):
                     onward_pair(to).start()
 
             for step in range(RING):
@@ -609,14 +609,14 @@
             @pl.when(jnp.logical_not(final_row))
             def _():
                 product_step(RING - 1)
-                for to in range(2):
+                for to in (tip, other):
                     onward_columns(to).start()
 
             @pl.when(final_row)
             def _():
                 start_state()
                 product_step(RING - 2)
-                for to in range(2):
+                for to in (tip, other):
                     @pl.when(jnp.logical_or(x != RING - 1, tip != to))
                     def _():
                         to_last(to).start()

time: 82.5 us -> 82.5 us (level)
  no operation moved by 1% of the time
where the time goes in v13:
time: 82.5 us; the launch traced here: 82.4 us
  Pallas kernels  80.4 us (97%)
  other arithmetic  1.31 us (2%)
    pallas_call x1, Pallas kernels, on_device(): pl.pallas_call(functools.partial(sweep, rows_total), out_shape=(jax.Shape...  80.4 us

profile of v13, /device:TPU:121, one launch (start us, length us, event | category | flops | bytes accessed | tf_op | source)
XLA Modules:
  0.0 82.4 jit_solution(6199070513841833283)
XLA Ops:
  0.6 0.0 copy-start
  0.6 0.0 copy-start.1
  0.7 80.4 %shard_map.59 = (f32[1,32,512]{2,1,0:T(8,128)S(1)}, f32[1,32,1024]{2,1,0:T(8,128)S(1)}) custom-call(bf16[1,1024,512]{2,1,0:T(8,128)(2,1)} %maps_hbm.1, f32[1,32,512]{2,1,0:T(8,128)} %tips_hbm.1, bf16[1,512,2048]{2,1,0:T(8,128)(2,1)} %spikes_hbm.1), custom_call_target="tpu_custom_call" | custom-call | tf_op jit(solution)/shard_map/pallas_call | solution.py:745
  81.0 0.0 copy-done
  81.1 0.6 add.3
  81.7 0.0 copy-done.1
  81.7 0.7 sub.3
Async XLA Ops:
  0.6 80.4 %copy-start = (f32[1,32,512]{2,1,0:T(8,128)S(1)}, f32[1,32,512]{2,1,0:T(8,128)}, u32[]{:S(2)}) copy-start(f32[1,32,512]{2,1,0:T(8,128)} %tips_hbm.1) | copy-start | bytes 196612
  0.6 81.1 %copy-start.1 = (f32[1,32,1024]{2,1,0:T(8,128)S(1)}, f32[1,32,1024]{2,1,0:T(8,128)}, u32[]{:S(2)}) copy-start(f32[1,32,1024]{2,1,0:T(8,128)} %param.7) | copy-start | bytes 393220

commit v14 on v13

--- a/solution.py
+++ b/solution.py
@@ -542,6 +542,32 @@
         def onward_columns(to):
             return remote(columns_out, columns_in.at[tip], wave_send.at[to], wave_recv.at[5 + tip], me + RING, to)
 
+        def drain():
+            @pl.when(jnp.logical_not(all_helped))
+            def _():
+                whole.drain()
+
+            for those, first, n, _, chip, in_chain in helping:
+                if not in_chain:
+                    @pl.when(those)
+                    def _():
+                        relay_drain(first, n, chip)
+
+            for (those, _, parts), gather in zip(helped, gathers):
+                @pl.when(those)
+                def _():
+                    gather.drain()
+                    for first, n, chip in parts:
+                        for k in range(first, first + n):
+                            to_relay(k, chip).wait_send()
+                            for step in range(1, RING):
+                                relayed_to_sibling(step, k).wait_send()
+
+            for part in range(2):
+                own_sibling_map(part).wait_send()
+            for number, (step, to) in enumerate(partners):
+                tip_copy(step, to, number).wait_send()
+
         @pl.when(direct)
         def _():
             remote(few_in, few_in, wave_send.at[0], wave_recv.at[2], me, other).wait_recv()
@@ -585,6 +611,10 @@
             @pl.when(final_row)
             def _():
                 prepare(RING - 2)
+
+            @pl.when(final_row)
+            def _():
+                drain()
 
             @pl.when(row == PRODUCT_ROW)
             def _():
@@ -666,30 +696,9 @@
             for piece in range(2 * RING):
                 full[piece * few : (piece + 1) * few, :] = prior[piece]
 
-        @pl.when(jnp.logical_not(all_helped))
-        def _():
-            whole.drain()
-
-        for those, first, n, _, chip, in_chain in helping:
-            if not in_chain:
-                @pl.when(those)
-                def _():
-                    relay_drain(first, n, chip)
-
-        for (those, _, parts), gather in zip(helped, gathers):
-            @pl.when(those)
-            def _():
-                gather.drain()
-                for first, n, chip in parts:
-                    for k in range(first, first + n):
-                        to_relay(k, chip).wait_send()
-                        for step in range(1, RING):
-                            relayed_to_sibling(step, k).wait_send()
-
-        for part in range(2):
-            own_sibling_map(part).wait_send()
-        for number, (step, to) in enumerate(partners):
-            tip_copy(step, to, number).wait_send()
+        @pl.when(jnp.logical_not(final_row))
+        def _():
+            drain()
 
         @pl.when(row < PRODUCT_ROW - 1)
         def _():

time: 82.5 us -> 82.3 us (level)
  no operation moved by 1% of the time
where the time goes in v14:
time: 82.3 us; the launch traced here: 82.2 us
  Pallas kernels  80.2 us (97%)
  other arithmetic  1.31 us (2%)
    pallas_call x1, Pallas kernels, on_device(): pl.pallas_call(functools.partial(sweep, rows_total), out_shape=(jax.Shape...  80.2 us

profile of v14, /device:TPU:121, one launch (start us, length us, event | category | flops | bytes accessed | tf_op | source)
XLA Modules:
  0.0 82.2 jit_solution(6190177622092641464)
XLA Ops:
  0.6 0.0 copy-start
  0.6 0.0 copy-start.1
  0.7 80.2 %shard_map.59 = (f32[1,32,512]{2,1,0:T(8,128)S(1)}, f32[1,32,1024]{2,1,0:T(8,128)S(1)}) custom-call(bf16[1,1024,512]{2,1,0:T(8,128)(2,1)} %maps_hbm.1, f32[1,32,512]{2,1,0:T(8,128)} %tips_hbm.1, bf16[1,512,2048]{2,1,0:T(8,128)(2,1)} %spikes_hbm.1), custom_call_target="tpu_custom_call" | custom-call | tf_op jit(solution)/shard_map/pallas_call | solution.py:754
  80.8 0.0 copy-done
  80.8 0.6 add.3
  81.5 0.0 copy-done.1
  81.5 0.7 sub.3
Async XLA Ops:
  0.6 80.2 %copy-start = (f32[1,32,512]{2,1,0:T(8,128)S(1)}, f32[1,32,512]{2,1,0:T(8,128)}, u32[]{:S(2)}) copy-start(f32[1,32,512]{2,1,0:T(8,128)} %tips_hbm.1) | copy-start | bytes 196612
  0.6 80.8 %copy-start.1 = (f32[1,32,1024]{2,1,0:T(8,128)S(1)}, f32[1,32,1024]{2,1,0:T(8,128)}, u32[]{:S(2)}) copy-start(f32[1,32,1024]{2,1,0:T(8,128)} %param.7) | copy-start | bytes 393220
